TPU v7x, 32 devices: a whole 2x2x4 slice. The times are simulated.
32 devices in a mesh: seq: 16 (over z, y, x), tp: 2 (over core).
Axes of the slice: x: 2, y: 2, z: 4, core: 2. Of those that a mesh axis runs over, the one named last changes fastest.
Arguments:
- tokens: bfloat16 [1088, 2048], P('seq'), may hold values from -6 to 6
- norm_gain: bfloat16 [2048], replicated, may hold values from 0.099609375 to 1.8984375
- w_query: bfloat16 [2048, 2048], P(None, 'tp'), may hold values from -0.125 to 0.125
- w_key: bfloat16 [2048, 1024], P(None, 'tp'), may hold values from -0.125 to 0.125
- w_value: bfloat16 [2048, 1024], P(None, 'tp'), may hold values from -0.125 to 0.125
- w_out: bfloat16 [2048, 2048], P('tp'), may hold values from -0.125 to 0.125
- cache_keys: bfloat16 [32768, 1024], P('seq', 'tp'), may hold values from -400 to 400
- cache_values: bfloat16 [32768, 1024], P('seq', 'tp'), may hold values from -6 to 6
- cached_len: int32 [66], replicated, may hold values from 1 to 4096, 32768 in all
- block_of_shard: int32 [16], P('seq'), may hold values from 0 to 15, each once
Outputs:
- mixed: bfloat16 [1088, 2048], P('seq', 'tp')
Inputs may be any that keep to these rules, and one draw needn't show every extreme that they name: `cached_len`: they sum to exactly 32768, so every cache slot belongs to a request; the largest is 4096. `block_of_shard`: each index of seq stores a different block.
All inputs are finite; a program needn't handle non-finite values.
Results may differ from a plain program's by a relative error of at most 0.02.
Values may be sent and summed in bfloat16 or wider, within the bound.
A program may use at most 192 MiB of HBM per device.

v0:
```python
import jax
import jax.numpy as jnp
from jax import lax
from jax.sharding import PartitionSpec as P

HD = 128
SPAN = 512
PREFILLS = 2


NEGATIVE = -1e30
THETA = 1000000.0
EPSILON = 1e-06


def rotate(values, places):
    half_dim = values.shape[-1] // 2
    frequency = THETA ** (-jnp.arange(half_dim, dtype=jnp.float32) / half_dim)
    angles = places.astype(jnp.float32)[:, None] * frequency[None, :]
    cosine = jnp.cos(angles)[:, None, :]
    sine_part = jnp.sin(angles)[:, None, :]
    front_half = values[..., :half_dim]
    second = values[..., half_dim:]
    return jnp.concatenate(
        [front_half * cosine - second * sine_part, second * cosine + front_half * sine_part],
        axis=-1,
    )


def row_layout(row_count, cached_len):
    position_index = jnp.arange(row_count, dtype=jnp.int32)
    boundary = PREFILLS * SPAN
    request = jnp.where(
        position_index < boundary, position_index // SPAN, PREFILLS + position_index - boundary
    )
    offset = jnp.where(position_index < boundary, position_index % SPAN, 0)
    matches = request[:, None] == jnp.arange(cached_len.shape[0], dtype=jnp.int32)[None, :]
    begins = jnp.sum(jnp.where(matches, cached_len[None, :], 0), axis=1)
    return (request, begins + offset)


def slot_layout(block_number, slot_count, cached_len):
    packed = block_number * slot_count + jnp.arange(slot_count, dtype=jnp.int32)
    ending = jnp.cumsum(cached_len)
    before = packed[:, None] >= ending[None, :]
    request = jnp.sum(before.astype(jnp.int32), axis=1)
    places = packed - jnp.sum(jnp.where(before, cached_len[None, :], 0), axis=1)
    return (request, places)


def per_device(
    tokens,
    norm_gain,
    w_query,
    w_key,
    w_value,
    w_out,
    cache_keys,
    cache_values,
    cached_len,
    block_of_shard,
):
    seq_count = lax.axis_size("seq")
    seq_index = lax.axis_index("seq")
    tok_rows = tokens.shape[0]
    all_rows = tok_rows * seq_count
    q_heads = w_query.shape[1] // HD
    kv_heads = w_key.shape[1] // HD
    head_groups = q_heads // kv_heads
    boundary = PREFILLS * SPAN
    request_all, position_all = row_layout(all_rows, cached_len)
    my_request = lax.dynamic_slice_in_dim(request_all, seq_index * tok_rows, tok_rows)
    my_position = lax.dynamic_slice_in_dim(position_all, seq_index * tok_rows, tok_rows)
    hidden = tokens.astype(jnp.float32)
    scale_row = lax.rsqrt(jnp.mean(hidden * hidden, axis=1, keepdims=True) + EPSILON)
    normed = (hidden * scale_row * norm_gain.astype(jnp.float32)[None, :]).astype(jnp.bfloat16)
    queries = jnp.dot(normed, w_query, preferred_element_type=jnp.float32).reshape(
        tok_rows, q_heads, HD
    )
    queries = rotate(queries, my_position).astype(jnp.bfloat16).reshape(tok_rows, q_heads * HD)
    new_keys = jnp.dot(normed, w_key, preferred_element_type=jnp.float32).reshape(
        tok_rows, kv_heads, HD
    )
    new_keys = rotate(new_keys, my_position).astype(jnp.bfloat16)
    new_values = (
        jnp.dot(normed, w_value, preferred_element_type=jnp.float32)
        .astype(jnp.bfloat16)
        .reshape(tok_rows, kv_heads, HD)
    )
    key_block = jnp.concatenate([cache_keys.reshape(-1, kv_heads, HD), new_keys], axis=0)
    value_block = jnp.concatenate([cache_values.reshape(-1, kv_heads, HD), new_values], axis=0)
    slot_request, slot_position = slot_layout(block_of_shard[0], cache_keys.shape[0], cached_len)
    key_request = jnp.concatenate([slot_request, my_request], axis=0)
    key_position = jnp.concatenate([slot_position, my_position], axis=0)
    gathered = lax.all_gather(queries, "seq", axis=0, tiled=True)

    def block_partial(block_item):
        q_rows, q_request, q_position = block_item
        row_count = q_rows.shape[0]
        q_four = q_rows.reshape(row_count, kv_heads, head_groups, HD)
        scores = jnp.einsum(
            "bcgd,kcd->bcgk", q_four, key_block, preferred_element_type=jnp.float32
        ) * HD ** (-0.5)
        visible = (q_request[:, None] == key_request[None, :]) & (
            key_position[None, :] <= q_position[:, None]
        )
        visible = visible[:, None, None, :]
        scores = jnp.where(visible, scores, NEGATIVE)
        row_top = jnp.max(scores, axis=-1)
        weights = jnp.where(visible, jnp.exp(scores - row_top[..., None]), 0.0)
        denominator = jnp.sum(weights, axis=-1)
        numerator = jnp.einsum(
            "bcgk,kcd->bcgd",
            weights.astype(jnp.bfloat16),
            value_block,
            preferred_element_type=jnp.float32,
        )
        return (
            row_top.reshape(row_count, q_heads),
            numerator.reshape(row_count, q_heads, HD),
            denominator.reshape(row_count, q_heads),
        )

    def prefill_block(block_item):
        return block_partial(block_item)

    prefill_parts = lax.map(
        prefill_block,
        (
            gathered[:boundary].reshape(PREFILLS, SPAN, q_heads * HD),
            request_all[:boundary].reshape(PREFILLS, SPAN),
            position_all[:boundary].reshape(PREFILLS, SPAN),
        ),
    )
    decode_parts = block_partial(
        (gathered[boundary:], request_all[boundary:], position_all[boundary:])
    )
    row_top = jnp.concatenate(
        [prefill_parts[0].reshape(boundary, q_heads), decode_parts[0]], axis=0
    )
    numerator = jnp.concatenate(
        [prefill_parts[1].reshape(boundary, q_heads, HD), decode_parts[1]], axis=0
    )
    denominator = jnp.concatenate(
        [prefill_parts[2].reshape(boundary, q_heads), decode_parts[2]], axis=0
    )
    overall = lax.pmax(row_top, "seq")
    factor = jnp.exp(row_top - overall)
    numerator, denominator = (
        lax.psum_scatter(numerator * factor[..., None], "seq", scatter_dimension=0, tiled=True),
        lax.psum_scatter(denominator * factor, "seq", scatter_dimension=0, tiled=True),
    )
    attended = (
        (numerator / denominator[..., None]).astype(jnp.bfloat16).reshape(tok_rows, q_heads * HD)
    )
    partial_out = jnp.dot(attended, w_out, preferred_element_type=jnp.float32)
    return lax.psum_scatter(partial_out.astype(jnp.bfloat16), "tp", scatter_dimension=1, tiled=True)


def solution(mesh):
    in_specs = (
        P("seq", None),
        P(),
        P(None, "tp"),
        P(None, "tp"),
        P(None, "tp"),
        P("tp", None),
        P("seq", "tp"),
        P("seq", "tp"),
        P(),
        P("seq"),
    )
    out_specs = P("seq", "tp")
    return jax.shard_map(
        per_device, mesh=mesh, in_specs=in_specs, out_specs=out_specs, check_vma=False
    )
```

profile of v0, /device:TPU:15, one launch (start us, length us, event | category | flops | bytes accessed | tf_op | source)
XLA Modules:
  0.0 405.6 jit_solution(447416544101258985)
XLA Ops:
  9.4 3.2 fusion.46
  15.8 2.1 fusion.44
  18.0 2.9 copy.49
  20.9 2.5 copy.52
  23.5 4.0 copy.53
  27.5 3.0 copy.54
  31.0 4.0 maximum_maximum_fusion
  35.2 41.2 %all-gather.3.cloned.1.call-done = bf16[16,68,1024]{2,1,0:T(8,128)(2,1)} async-done(((bf16[1,68,1024]{2,1,0:T(8,128)(2,1)}), bf16[16,68,1024]{2,1,0:T(8,128)(2,1)}) %all-gather.3.cloned.1.call-update) | async-done | bytes 2228240 | tf_op jit(solution)/shard_map/all_gather | solution.py:95
  76.4 4.0 reshape.295
  80.4 3.1 slice.44
  83.6 2.8 fusion.50
  86.4 1.8 fusion.18
  88.2 1.6 fusion.16
  89.9 113.3 %while.14 = (s32[]{:T(128)}, f32[2,512,8]{1,2,0:T(8,128)S(1)}, f32[2,512,8,128]{3,2,1,0:T(8,128)}, f32[2,512,8]{1,2,0:T(8,128)S(1)}, s32[2,512]{1,0:T(2,128)S(1)...) while((s32[]{:T(128)}, f32[2,512,8]{1,2,0:T(8,128)S(1)}, ...), condition=%wide.region_8.9_spmd, body=%wide.region_5.8_spmd.sunk | while | flops 4553488384 | bytes 133100232 | solution.py:127
  89.9 1.3 constant_dynamic-slice_fusion.9
  91.8 1.6 compare_and_fusion.3
  93.4 15.7 %bitcast_reduce_fusion.2 = (f32[512,4,2]{0,2,1:T(2,128)S(1)}, f32[4,512,2,2116]{1,3,2,0:T(8,128)}) fusion(pred[512,2116]{0,1:T(8,128)(4,1)S(1)} %compare_and_fusion.3, bf16[512,4,2,128]{0,3,2,1:T(8,128)(2,1)S(1)} %bitcast.99, bf16[2116,4,128]{2,0,1:T(8,128)(2,1)} %get-tuple-element.254), kind=kOutput, calls=%fused_computation.1.clone.1 | convolution fusion | flops 2244784128 | bytes 38983680 | tf_op jit(solution)/shard_map/while/body/eval_jaxpr/bcgd,kcd->bcgk/dot_general | solution.py:101
  109.1 15.3 %fusion.65 = f32[512,4,2]{0,2,1:T(2,128)S(1)} fusion(f32[4,512,2,2116]{1,3,2,0:T(8,128)} %get-tuple-element.217, f32[512,4,2]{0,2,1:T(2,128)S(1)} %get-tuple-element.218, pred[512,2116]{0,1:T(8,128)(4,1)S(1)} %compare_and_fusion.3), kind=kLoop, calls=%fused_computation.5.clone.1 | loop fusion | flops 43331584 | bytes 35784704 | tf_op jit(solution)/shard_map/while/body/eval_jaxpr/reduce_sum | solution.py:111
  124.4 18.0 %fusion.66 = f32[4,512,2,128]{3,1,2,0:T(8,128)} fusion(f32[4,512,2,2116]{1,3,2,0:T(8,128)} %get-tuple-element.217, f32[512,4,2]{0,2,1:T(2,128)S(1)} %get-tuple-element.218, pred[512,2116]{0,1:T(8,128)(4,1)S(1)} %compare_and_fusion.3, bf16[2116,4,128]{2,0,1:T(8,128)(2,1)S(1)} %copy-done.5), kind=kOutput, calls=%fused_computation.7.clone.1 | convolution fusion | flops 2262122496 | bytes 40032256 | tf_op jit(solution)/shard_map/while/body/eval_jaxpr/bcgk,kcd->bcgd/dot_general | solution.py:112
  142.4 4.1 %copy_dynamic-update-slice_fusion.2 = f32[2,512,8,128]{3,2,1,0:T(8,128)} fusion(f32[2,512,8,128]{3,2,1,0:T(8,128)} %get-tuple-element.235, s32[]{:T(128)S(6)} %copy.98, f32[1,512,8,128]{3,1,2,0:T(8,128)} %bitcast.98), kind=kLoop, calls=%fused_computation.14.clone.1 | loop fusion | bytes 4194308 | tf_op jit(solution)/shard_map/while/body/jit(dynamic_update_index_in_dim)/dynamic_update_slice | solution.py:127
  146.6 1.3 constant_dynamic-slice_fusion.9
  148.4 1.6 compare_and_fusion.3
  150.0 15.7 %bitcast_reduce_fusion.2 = (f32[512,4,2]{0,2,1:T(2,128)S(1)}, f32[4,512,2,2116]{1,3,2,0:T(8,128)}) fusion(pred[512,2116]{0,1:T(8,128)(4,1)S(1)} %compare_and_fusion.3, bf16[512,4,2,128]{0,3,2,1:T(8,128)(2,1)S(1)} %bitcast.99, bf16[2116,4,128]{2,0,1:T(8,128)(2,1)} %get-tuple-element.254), kind=kOutput, calls=%fused_computation.1.clone.1 | convolution fusion | flops 2244784128 | bytes 38983680 | tf_op jit(solution)/shard_map/while/body/eval_jaxpr/bcgd,kcd->bcgk/dot_general | solution.py:101
  165.7 15.3 %fusion.65 = f32[512,4,2]{0,2,1:T(2,128)S(1)} fusion(f32[4,512,2,2116]{1,3,2,0:T(8,128)} %get-tuple-element.217, f32[512,4,2]{0,2,1:T(2,128)S(1)} %get-tuple-element.218, pred[512,2116]{0,1:T(8,128)(4,1)S(1)} %compare_and_fusion.3), kind=kLoop, calls=%fused_computation.5.clone.1 | loop fusion | flops 43331584 | bytes 35784704 | tf_op jit(solution)/shard_map/while/body/eval_jaxpr/reduce_sum | solution.py:111
  181.0 18.0 %fusion.66 = f32[4,512,2,128]{3,1,2,0:T(8,128)} fusion(f32[4,512,2,2116]{1,3,2,0:T(8,128)} %get-tuple-element.217, f32[512,4,2]{0,2,1:T(2,128)S(1)} %get-tuple-element.218, pred[512,2116]{0,1:T(8,128)(4,1)S(1)} %compare_and_fusion.3, bf16[2116,4,128]{2,0,1:T(8,128)(2,1)S(1)} %copy-done.5), kind=kOutput, calls=%fused_computation.7.clone.1 | convolution fusion | flops 2262122496 | bytes 40032256 | tf_op jit(solution)/shard_map/while/body/eval_jaxpr/bcgk,kcd->bcgd/dot_general | solution.py:112
  199.0 4.2 %copy_dynamic-update-slice_fusion.2 = f32[2,512,8,128]{3,2,1,0:T(8,128)} fusion(f32[2,512,8,128]{3,2,1,0:T(8,128)} %get-tuple-element.235, s32[]{:T(128)S(6)} %copy.98, f32[1,512,8,128]{3,1,2,0:T(8,128)} %bitcast.98), kind=kLoop, calls=%fused_computation.14.clone.1 | loop fusion | bytes 4194308 | tf_op jit(solution)/shard_map/while/body/jit(dynamic_update_index_in_dim)/dynamic_update_slice | solution.py:127
  203.4 47.1 %pmax.7 = f32[1088,8]{0,1:T(8,128)S(1)} all-reduce(f32[1088,8]{0,1:T(8,128)S(1)} %pad_maximum_fusion.2), channel_id=1, replica_groups=mesh['seq'=16,'tp'=2] {'seq'}, use_global_device_ids=true, to_apply=%region_10.11 | all-reduce | flops 8704 | bytes 69632 | tf_op jit(solution)/shard_map/pmax | solution.py:147
  250.7 7.4 %maximum_multiply_fusion = f32[1088,8,128]{2,1,0:T(8,128)} fusion(f32[64,8,128]{2,1,0:T(8,128)S(1)} %copy.59, f32[1024,8,128]{2,1,0:T(8,128)} %bitcast.103, f32[1088,8]{1,0:T(8,128)S(1)} %copy.60), kind=kLoop, calls=%fused_computation.26 | loop fusion | flops 2228224 | bytes 8947712 | tf_op jit(solution)/shard_map/mul | solution.py:150
  260.0 66.8 %all-reduce = f32[1088,8]{0,1:T(8,128)S(1)} all-reduce(f32[1088,8]{0,1:T(8,128)S(1)} %get-tuple-element.124), channel_id=3, replica_groups=mesh['seq'=16,'tp'=2] {'seq'}, use_global_device_ids=true, to_apply=%region_13.14.clone | all-reduce | flops 8704 | bytes 69632
  327.0 56.8 %reduce-scatter.4.cloned.1.call-done = f32[68,8,128]{2,1,0:T(8,128)} async-done(((f32[1088,8,128]{2,1,0:T(8,128)}), f32[68,8,128]{2,1,0:T(8,128)}) %reduce-scatter.4.cloned.1.call-update) | async-done | bytes 278544 | tf_op jit(solution)/shard_map/reduce_scatter | solution.py:150
  384.9 3.8 convolution_convert_fusion
  388.7 10.4 %reduce-scatter.6.cloned.1.call-done = bf16[68,1024]{1,0:T(8,128)(2,1)} async-done(((bf16[68,2048]{1,0:T(8,128)(2,1)}), bf16[68,1024]{1,0:T(8,128)(2,1)}) %reduce-scatter.6.cloned.1.call-update) | async-done | bytes 139280 | tf_op jit(solution)/shard_map/reduce_scatter | solution.py:157
  (101 shorter events, 10.1 us)
Async XLA Ops:
  6.5 8.6 %copy-start = (bf16[2048,512]{1,0:T(8,128)(2,1)S(1)}, bf16[2048,512]{1,0:T(8,128)(2,1)}, u32[]{:S(2)}) copy-start(bf16[2048,512]{1,0:T(8,128)(2,1)} %param.16) | copy-start | bytes 6291460
  6.5 8.6 %copy-start.4 = (bf16[68,2048]{1,0:T(8,128)(2,1)S(1)}, bf16[68,2048]{1,0:T(8,128)(2,1)}, u32[]{:S(2)}) copy-start(bf16[68,2048]{1,0:T(8,128)(2,1)} %param.12) | copy-start | bytes 835588
  6.5 8.3 %copy-start.12 = (s32[66]{0:T(128)S(1)}, s32[66]{0:T(128)}, u32[]{:S(2)}) copy-start(s32[66]{0:T(128)} %param.20) | copy-start | bytes 796
  6.5 69.8 %all-gather.3.cloned.1.call-start = ((), (), s32[]{:S(2)}) async-start(), calls=%async_computation.4 | async-start | bytes 2506752 | tf_op jit(solution)/shard_map/all_gather | solution.py:95
  6.6 9.2 %copy-start.9 = (s32[1088]{0:T(1024)}, s32[1088]{0:T(1024)S(1)}, u32[]{:S(2)}) copy-start(s32[1088]{0:T(1024)S(1)} %fusion.36) | copy-start | bytes 13060
  8.7 7.1 %copy-start.10 = (s32[1088]{0:T(1024)}, s32[1088]{0:T(1024)S(1)}, u32[]{:S(2)}) copy-start(s32[1088]{0:T(1024)S(1)} %fusion.39) | copy-start | bytes 13060
  14.0 369.7 %reduce-scatter.4.cloned.1.call-start = ((), (), s32[]{:S(2)}) async-start(), calls=%async_computation.2 | async-start | bytes 4734976 | tf_op jit(solution)/shard_map/reduce_scatter | solution.py:150
  30.5 4.5 %copy-start.2 = (bf16[2048,4,128]{2,0,1:T(8,128)(2,1)}, bf16[2048,4,128]{2,0,1:T(8,128)(2,1)S(1)}, u32[]{:S(2)}) copy-start(bf16[2048,4,128]{2,0,1:T(8,128)(2,1)S(1)} %copy.54) | copy-start | bytes 6291460
  31.0 4.0 slice-start.1
  31.0 4.0 slice-start.2
  80.4 3.1 slice-start
  83.6 2.8 copy-start.3
  86.4 1.8 copy-start.7
  89.9 113.3 %copy-start.6 = (f32[4,128,64,2]{1,2,3,0:T(8,128)S(1)}, f32[4,128,64,2]{1,2,3,0:T(8,128)}, u32[]{:S(2)}) copy-start(f32[4,128,64,2]{1,2,3,0:T(8,128)} %fusion.18) | copy-start | bytes 786436
  89.9 113.5 %copy-start.8 = (f32[64,4,2]{0,2,1:T(2,128)S(1)}, f32[64,4,2]{0,2,1:T(2,128)}, u32[]{:S(2)}) copy-start(f32[64,4,2]{0,2,1:T(2,128)} %copy-done.7) | copy-start | bytes 6148
  89.9 160.6 %copy-start.11 = (f32[64,4,2]{0,2,1:T(2,128)S(1)}, f32[64,4,2]{0,2,1:T(2,128)}, u32[]{:S(2)}) copy-start(f32[64,4,2]{0,2,1:T(2,128)} %fusion.16) | copy-start | bytes 6148
  109.1 15.3 %copy-start.5 = (bf16[2116,4,128]{2,0,1:T(8,128)(2,1)S(1)}, bf16[2116,4,128]{2,0,1:T(8,128)(2,1)}, u32[]{:S(2)}) copy-start(bf16[2116,4,128]{2,0,1:T(8,128)(2,1)} %get-tuple-element.255) | copy-start | bytes 6500356 | tf_op jit(solution)/shard_map/while
  165.7 15.3 %copy-start.5 = (bf16[2116,4,128]{2,0,1:T(8,128)(2,1)S(1)}, bf16[2116,4,128]{2,0,1:T(8,128)(2,1)}, u32[]{:S(2)}) copy-start(bf16[2116,4,128]{2,0,1:T(8,128)(2,1)} %get-tuple-element.255) | copy-start | bytes 6500356 | tf_op jit(solution)/shard_map/while
  258.1 0.7 copy-start.13
  258.1 141.0 %copy-start.1 = (bf16[2048,512]{1,0:T(8,128)(2,1)S(1)}, bf16[2048,512]{1,0:T(8,128)(2,1)}, u32[]{:S(2)}) copy-start(bf16[2048,512]{1,0:T(8,128)(2,1)} %param.16) | copy-start | bytes 6291460
  258.1 141.0 %reduce-scatter.6.cloned.1.call-start = ((), (), s32[]{:S(2)}) async-start(), calls=%async_computation.3 | async-start | bytes 442368 | tf_op jit(solution)/shard_map/reduce_scatter | solution.py:157
Sparse Core Ops, SparseCore 0:
  14.1 62.1 all-gather.2
  258.2 125.4 reduce-scatter.3
  388.8 10.2 reduce-scatter.5
where the time goes:
time: 408 us; the launch traced here: 406 us
  blocking collectives  114 us (28%)
  waiting for transfers between devices  108 us (26%)
  matrix products  81.5 us (20%)
  other arithmetic  51.9 us (13%)
  local copies, waits for them, and re-layouts  34.9 us (9%)
  between operations  14.8 us (4%)
    unnamed x1, blocking collectives  66.8 us
    reduce_scatter x1, waiting for transfers between devices, per_device(): lax.psum_scatter(numerator * factor[..., None], 'seq', scatter_dimension=...  56.8 us
    pmax x1, blocking collectives, per_device(): overall = lax.pmax(row_top, 'seq')  47.1 us
    all_gather x1, waiting for transfers between devices, per_device(): gathered = lax.all_gather(queries, 'seq', axis=0, tiled=True)  41.2 us
    dot_general x3, matrix products, block_partial(): jnp.einsum('bcgk,kcd->bcgd', weights.astype(jnp.bfloat16), value_block, p...  37.7 us
    dot_general x3, matrix products, block_partial(): jnp.einsum('bcgd,kcd->bcgk', q_four, key_block, preferred_element_type=jn...  34.1 us
    reduce_sum x3, other arithmetic, block_partial(): denominator = jnp.sum(weights, axis=-1)  32.3 us
    unnamed x35, local copies, waits for them, and re-layouts  13.1 us
  transfers between devices with their start and end apart: 3, of which 3 were waited for; matrix products, arithmetic and copies ran while one was open for 5% of the time, Pallas kernels for 0%

commit v1 on v0

v1 whole, which is shorter than its diff:
```python
import functools

import jax
import jax.numpy as jnp
from jax import lax
from jax.experimental import pallas as pl
from jax.experimental.pallas import tpu as pltpu
from jax.sharding import PartitionSpec as P

HD = 128
SPAN = 512
PREFILLS = 2
TILE = 256
NEGATIVE = -1e30
THETA = 1000000.0
EPSILON = 1e-06
SCALE = HD ** (-0.5)


def rotate(values, places):
    half_dim = values.shape[-1] // 2
    frequency = THETA ** (-jnp.arange(half_dim, dtype=jnp.float32) / half_dim)
    angles = places.astype(jnp.float32)[:, None] * frequency[None, :]
    cosine = jnp.cos(angles)[:, None, :]
    sine_part = jnp.sin(angles)[:, None, :]
    front_half = values[..., :half_dim]
    second = values[..., half_dim:]
    return jnp.concatenate(
        [front_half * cosine - second * sine_part, second * cosine + front_half * sine_part],
        axis=-1,
    )


def nt_dot(a, b):
    return lax.dot_general(a, b, (((1,), (1,)), ((), ())), preferred_element_type=jnp.float32)


def tn_dot(a, b):
    return lax.dot_general(a, b, (((0,), (0,)), ((), ())), preferred_element_type=jnp.float32)


def tile_step(q, k, v, lo, hi, first, state, top_ref, sum_ref, acc_ref, width):
    scores = nt_dot(k, q) * SCALE
    index = first + lax.broadcasted_iota(jnp.int32, scores.shape, 0)
    visible = (index >= lo) & (index < hi)
    scores = jnp.where(visible, scores, NEGATIVE)
    old = top_ref[:, :width]
    top = jnp.maximum(old, jnp.max(scores, axis=0, keepdims=True))
    weights = jnp.where(visible, jnp.exp(scores - top), 0.0)
    factor = jnp.exp(old - top)
    top_ref[:, :width] = top
    sum_ref[:, :width] = sum_ref[:, :width] * factor + jnp.sum(weights, axis=0, keepdims=True)
    acc_ref[:, :width] = acc_ref[:, :width] * factor + tn_dot(v, weights.astype(jnp.bfloat16))


def begin(top_ref, sum_ref, acc_ref):
    top_ref[...] = jnp.full(top_ref.shape, NEGATIVE, jnp.float32)
    sum_ref[...] = jnp.zeros(sum_ref.shape, jnp.float32)
    acc_ref[...] = jnp.zeros(acc_ref.shape, jnp.float32)


def finish(top_ref, sum_ref, acc_ref, width):
    total = sum_ref[:, :width]
    some = total > 0.0
    safe = jnp.where(some, total, 1.0)
    out = acc_ref[:, :width] / safe
    return out, jnp.where(some, top_ref[:, :width] + jnp.log(safe), NEGATIVE)


def cache_kernel(range_ref, lo_ref, hi_ref, q_ref, k_ref, v_ref, o_ref, l_ref, top_ref, sum_ref, acc_ref):
    groups = q_ref.shape[1] // HD
    boundary = PREFILLS * SPAN
    decodes = q_ref.shape[0] - boundary
    tiles = k_ref.shape[0] // TILE

    def attend(q, lo, hi, first_tile, last_tile, width):
        begin(top_ref, sum_ref, acc_ref)

        @pl.loop(first_tile, last_tile)
        def _(tile):
            first = pl.multiple_of(tile * TILE, TILE)
            tile_step(
                q, k_ref[pl.ds(first, TILE), :], v_ref[pl.ds(first, TILE), :],
                lo, hi, first, None, top_ref, sum_ref, acc_ref, width,
            )

        return finish(top_ref, sum_ref, acc_ref, width)

    q = jnp.concatenate(
        [q_ref[boundary:, g * HD:(g + 1) * HD] for g in range(groups)], axis=0
    )
    out, lse = attend(q, lo_ref[...], hi_ref[...], 0, tiles, groups * decodes)
    out = out.T.astype(jnp.bfloat16)
    for g in range(groups):
        o_ref[boundary:, g * HD:(g + 1) * HD] = out[g * decodes:(g + 1) * decodes]
        l_ref[0, g:g + 1, boundary:] = lse[:, g * decodes:(g + 1) * decodes]
    for r in range(PREFILLS):
        lo, hi = range_ref[2 * r], range_ref[2 * r + 1]
        rows = slice(r * SPAN, (r + 1) * SPAN)

        @pl.when(hi > lo)
        def _():
            for g in range(groups):
                q = q_ref[rows, g * HD:(g + 1) * HD]
                out, lse = attend(q, lo, hi, lo // TILE, (hi + TILE - 1) // TILE, SPAN)
                o_ref[rows, g * HD:(g + 1) * HD] = out.T.astype(jnp.bfloat16)
                l_ref[0, g:g + 1, rows] = lse

        @pl.when(hi <= lo)
        def _():
            o_ref[rows, :] = jnp.zeros((SPAN, groups * HD), jnp.bfloat16)
            l_ref[0, :, rows] = jnp.full((groups, SPAN), NEGATIVE, jnp.float32)


def cache_attention(ranges, lo, hi, queries, keys, values):
    rows, q_width = queries.shape
    slots, kv_width = keys.shape
    kv_heads = kv_width // HD
    groups = q_width // kv_width
    whole = lambda c: (0, 0)
    column = lambda c: (0, c)
    return pl.pallas_call(
        cache_kernel,
        name="cache_attention",
        grid=(kv_heads,),
        out_shape=(
            jax.ShapeDtypeStruct((rows, q_width), jnp.bfloat16),
            jax.ShapeDtypeStruct((kv_heads, groups, rows), jnp.float32),
        ),
        in_specs=[
            pl.BlockSpec(memory_space=pltpu.SMEM),
            pl.BlockSpec(lo.shape, whole),
            pl.BlockSpec(hi.shape, whole),
            pl.BlockSpec((rows, groups * HD), column),
            pl.BlockSpec((slots, HD), column),
            pl.BlockSpec((slots, HD), column),
        ],
        out_specs=(
            pl.BlockSpec((rows, groups * HD), column),
            pl.BlockSpec((1, groups, rows), lambda c: (c, 0, 0)),
        ),
        scratch_shapes=[
            pltpu.VMEM((1, SPAN), jnp.float32),
            pltpu.VMEM((1, SPAN), jnp.float32),
            pltpu.VMEM((HD, SPAN), jnp.float32),
        ],
        compiler_params=pltpu.CompilerParams(vmem_limit_bytes=32 << 20),
        cost_estimate=pl.CostEstimate(
            flops=4 * slots * q_width * 512, bytes_accessed=8 << 20, transcendentals=1 << 20
        ),
    )(ranges, lo, hi, queries, keys, values)


def self_kernel(lo_ref, hi_ref, q_ref, k_ref, v_ref, o_ref, l_ref):
    groups = q_ref.shape[1] // HD
    keys, values = k_ref[...], v_ref[...]
    for g in range(groups):
        scores = nt_dot(keys, q_ref[:, g * HD:(g + 1) * HD]) * SCALE
        index = lax.broadcasted_iota(jnp.int32, scores.shape, 0)
        visible = (index >= lo_ref[...]) & (index <= hi_ref[...])
        scores = jnp.where(visible, scores, NEGATIVE)
        top = jnp.max(scores, axis=0, keepdims=True)
        weights = jnp.where(visible, jnp.exp(scores - top), 0.0)
        total = jnp.sum(weights, axis=0, keepdims=True)
        out = tn_dot(values, weights.astype(jnp.bfloat16)) / total
        o_ref[:, g * HD:(g + 1) * HD] = out.T
        l_ref[0, g:g + 1, :] = top + jnp.log(total)


def self_attention(lo, hi, queries, new):
    rows, q_width = queries.shape
    count, width = new.shape
    kv_heads = width // (2 * HD)
    groups = q_width // HD // kv_heads
    return pl.pallas_call(
        self_kernel,
        name="new_row_attention",
        grid=(kv_heads,),
        out_shape=(
            jax.ShapeDtypeStruct((rows, q_width), jnp.float32),
            jax.ShapeDtypeStruct((kv_heads, groups, rows), jnp.float32),
        ),
        in_specs=[
            pl.BlockSpec(lo.shape, lambda c: (0, 0)),
            pl.BlockSpec(hi.shape, lambda c: (0, 0)),
            pl.BlockSpec((rows, groups * HD), lambda c: (0, c)),
            pl.BlockSpec((count, HD), lambda c: (0, c)),
            pl.BlockSpec((count, HD), lambda c: (0, kv_heads + c)),
        ],
        out_specs=(
            pl.BlockSpec((rows, groups * HD), lambda c: (0, c)),
            pl.BlockSpec((1, groups, rows), lambda c: (c, 0, 0)),
        ),
        compiler_params=pltpu.CompilerParams(vmem_limit_bytes=32 << 20),
        cost_estimate=pl.CostEstimate(
            flops=4 * count * q_width * rows, bytes_accessed=4 << 20, transcendentals=1 << 20
        ),
    )(lo, hi, queries, new, new)


def per_device(
    tokens,
    norm_gain,
    w_query,
    w_key,
    w_value,
    w_out,
    cache_keys,
    cache_values,
    cached_len,
    block_of_shard,
):
    seq_count = lax.axis_size("seq")
    seq_index = lax.axis_index("seq")
    tok_rows = tokens.shape[0]
    all_rows = tok_rows * seq_count
    q_heads = w_query.shape[1] // HD
    kv_heads = w_key.shape[1] // HD
    groups = q_heads // kv_heads
    slots = cache_keys.shape[0]
    requests = cached_len.shape[0]
    boundary = PREFILLS * SPAN

    number = jnp.arange(requests, dtype=jnp.int32)
    ends = jnp.sum(jnp.where(number[None, :] <= number[:, None], cached_len[None, :], 0), axis=1)
    base = block_of_shard[0] * slots
    lows = jnp.clip(ends - cached_len - base, 0, slots)
    highs = jnp.clip(ends - base, 0, slots)
    ranges = jnp.stack([lows[:PREFILLS], highs[:PREFILLS]], axis=1).reshape(-1)
    decode_lo = jnp.tile(lows[PREFILLS:], groups)[None, :]
    decode_hi = jnp.tile(highs[PREFILLS:], groups)[None, :]

    my_rows = seq_index * tok_rows + jnp.arange(tok_rows, dtype=jnp.int32)
    prefill = my_rows < boundary
    my_request = jnp.where(prefill, my_rows // SPAN, PREFILLS + my_rows - boundary)
    my_begin = jnp.sum(
        jnp.where(my_request[:, None] == number[None, :], cached_len[None, :], 0), axis=1
    )
    my_position = my_begin + jnp.where(prefill, my_rows % SPAN, 0)

    hidden = tokens.astype(jnp.float32)
    scale_row = lax.rsqrt(jnp.mean(hidden * hidden, axis=1, keepdims=True) + EPSILON)
    normed = (hidden * scale_row * norm_gain.astype(jnp.float32)[None, :]).astype(jnp.bfloat16)
    queries = jnp.dot(normed, w_query, preferred_element_type=jnp.float32).reshape(
        tok_rows, q_heads, HD
    )
    queries = rotate(queries, my_position).astype(jnp.bfloat16).reshape(tok_rows, q_heads * HD)
    new_keys = jnp.dot(normed, w_key, preferred_element_type=jnp.float32).reshape(
        tok_rows, kv_heads, HD
    )
    new_keys = rotate(new_keys, my_position).astype(jnp.bfloat16).reshape(tok_rows, kv_heads * HD)
    new_values = jnp.dot(normed, w_value, preferred_element_type=jnp.float32).astype(jnp.bfloat16)
    gathered = lax.all_gather(queries, "seq", axis=0, tiled=True)
    new = lax.all_gather(
        jnp.concatenate([new_keys, new_values], axis=1), "seq", axis=0, tiled=True
    )

    part, part_lse = cache_attention(
        ranges, decode_lo, decode_hi, gathered, cache_keys, cache_values
    )
    part_lse = part_lse.reshape(q_heads, all_rows)
    every_lse = lax.all_gather(part_lse, "seq", axis=0)
    most = jnp.max(every_lse, axis=0)
    cache_lse = most + jnp.log(jnp.sum(jnp.exp(every_lse - most[None]), axis=0))
    share = jnp.where(part_lse > 0.5 * NEGATIVE, jnp.exp(part_lse - cache_lse), 0.0)
    part = part.reshape(all_rows, q_heads, HD).astype(jnp.float32) * share.T[:, :, None]
    part = part.astype(jnp.bfloat16).reshape(seq_count, tok_rows, q_heads * HD)
    cached = lax.psum_scatter(part, "seq", scatter_dimension=0)

    padded = -(-tok_rows // 128) * 128
    lane_rows = seq_index * tok_rows + jnp.minimum(
        jnp.arange(padded, dtype=jnp.int32), tok_rows - 1
    )
    first_key = jnp.where(lane_rows < boundary, lane_rows // SPAN * SPAN, lane_rows)
    own, own_lse = self_attention(
        first_key[None, :],
        lane_rows[None, :],
        jnp.pad(queries, ((0, padded - tok_rows), (0, 0))),
        new,
    )
    own = own[:tok_rows].reshape(tok_rows, q_heads, HD)
    own_lse = own_lse.reshape(q_heads, padded)[:, :tok_rows]
    my_cache_lse = lax.dynamic_slice_in_dim(cache_lse, seq_index * tok_rows, tok_rows, axis=1)
    top = jnp.maximum(own_lse, my_cache_lse)
    own_weight = jnp.exp(own_lse - top)
    cache_weight = jnp.exp(my_cache_lse - top)
    norm = own_weight + cache_weight
    own_weight = (own_weight / norm).T[:, :, None]
    cache_weight = (cache_weight / norm).T[:, :, None]
    cached = cached.reshape(tok_rows, q_heads, HD).astype(jnp.float32)
    attended = (own * own_weight + cached * cache_weight).astype(jnp.bfloat16)
    attended = attended.reshape(tok_rows, q_heads * HD)
    partial_out = jnp.dot(attended, w_out, preferred_element_type=jnp.float32)
    return lax.psum_scatter(partial_out.astype(jnp.bfloat16), "tp", scatter_dimension=1, tiled=True)


def solution(mesh):
    in_specs = (
        P("seq", None),
        P(),
        P(None, "tp"),
        P(None, "tp"),
        P(None, "tp"),
        P("tp", None),
        P("seq", "tp"),
        P("seq", "tp"),
        P(),
        P("seq"),
    )
    out_specs = P("seq", "tp")
    return jax.shard_map(
        per_device, mesh=mesh, in_specs=in_specs, out_specs=out_specs, check_vma=False
    )
```

time: 408 us -> 325 us (0.80); the launches traced: 406 us -> 328 us
  waiting for transfers between devices: 108 us -> 188 us
  matrix products: 81.5 us -> 9.68 us
  blocking collectives: 114 us -> 52.9 us
  other arithmetic: 51.9 us -> 10.7 us
  Pallas kernels: 0 us -> 20 us
    dot_general x6 -> x0, matrix products: 71.8 us -> none  [the longest x3 37.7 us: block_partial(): jnp.einsum('bcgk,kcd->bcgd', weights.astype(jnp.bfloat16), value_block, p...]
    unnamed x1 -> x0, blocking collectives: 66.8 us -> none
    reduce_scatter x1, waiting for transfers between devices: 56.8 us -> 122 us  [per_device(): cached = lax.psum_scatter(part, 'seq', scatter_dimension=0)]
    all_gather x0 -> x1, blocking collectives: none -> 52.9 us  [per_device(): every_lse = lax.all_gather(part_lse, 'seq', axis=0)]
    pmax x1 -> x0, blocking collectives: 47.1 us -> none  [per_device(): overall = lax.pmax(row_top, 'seq')]
    reduce_sum x5 -> x3, other arithmetic: 33.3 us -> 1.09 us  [the longest x1 0.89 us: per_device(): jnp.sum(jnp.where(my_request[:, None] == number[None, :], cached_len[None...]
    pallas_call x0 -> x2, Pallas kernels: none -> 20 us  [the longest x1 14.6 us: cache_attention(): pl.pallas_call(cache_kernel, name='cache_attention', grid=(kv_heads,), ou...]
    all_gather x1, waiting for transfers between devices: 41.2 us -> 57.1 us  [per_device(): gathered = lax.all_gather(queries, 'seq', axis=0, tiled=True)]
  transfers between devices with their start and end apart: 3 -> 4, of which waited for: 3 -> 3; matrix products, arithmetic and copies ran while one was open for 5% -> 10% of each run, Pallas kernels for 0% -> 6%
where the time goes in v1:
time: 325 us; the launch traced here: 328 us
  waiting for transfers between devices  188 us (58%)
  blocking collectives  52.9 us (16%)
  local copies, waits for them, and re-layouts  31.9 us (10%)
  Pallas kernels  20 us (6%)
  between operations  14.1 us (4%)
  other arithmetic  10.7 us (3%)
  matrix products  9.68 us (3%)
    reduce_scatter x1, waiting for transfers between devices, per_device(): cached = lax.psum_scatter(part, 'seq', scatter_dimension=0)  122 us
    all_gather x1, waiting for transfers between devices, per_device(): gathered = lax.all_gather(queries, 'seq', axis=0, tiled=True)  57.1 us
    all_gather x1, blocking collectives, per_device(): every_lse = lax.all_gather(part_lse, 'seq', axis=0)  52.9 us
    unnamed x28, local copies, waits for them, and re-layouts  16.9 us
    pallas_call x1, Pallas kernels, cache_attention(): pl.pallas_call(cache_kernel, name='cache_attention', grid=(kv_heads,), ou...  14.6 us
    reduce_scatter x1, waiting for transfers between devices, per_device(): lax.psum_scatter(partial_out.astype(jnp.bfloat16), 'tp', scatter_dimensio...  9.36 us
    mul x2, local copies, waits for them, and re-layouts, per_device(): part.reshape(all_rows, q_heads, HD).astype(jnp.float32)  9.1 us
  transfers between devices with their start and end apart: 4, of which 3 were waited for; matrix products, arithmetic and copies ran while one was open for 10% of the time, Pallas kernels for 6%

profile of v1, /device:TPU:15, one launch (start us, length us, event | category | flops | bytes accessed | tf_op | source)
XLA Modules:
  0.0 327.8 jit_solution(17107886450249718354)
XLA Ops:
  6.6 0.9 select_reduce_fusion.1
  7.5 0.7 convert_element_type.58
  8.2 1.1 fusion
  9.3 3.2 fusion.16
  12.6 0.2 multiply_cosine_fusion
  12.8 0.2 subtract_convert_fusion
  13.1 0.7 reshape.219
  14.0 0.5 fusion.14
  14.6 0.2 subtract_convert_fusion.1
  14.9 2.1 convolution_convert_fusion.1
  17.1 0.7 maximum_bitcast_fusion
  19.1 57.1 %all-gather.7.cloned.1.call-done = bf16[16,68,1024]{2,1,0:T(8,128)(2,1)} async-done(((bf16[1,68,1024]{2,1,0:T(8,128)(2,1)}), bf16[16,68,1024]{2,1,0:T(8,128)(2,1)}) %all-gather.7.cloned.1.call-update) | async-done | bytes 2228240 | tf_op jit(solution)/shard_map/all_gather | solution.py:253
  76.3 4.0 %reshape.220.q_ref = bf16[1088,1024]{1,0:T(8,128)(2,1)} reshape(bf16[16,68,1024]{2,1,0:T(8,128)(2,1)} %all-gather.7.cloned.1.call-done) | data formatting | bytes 4456448
  80.3 1.6 copy-done.2
  81.9 1.6 copy-done.4
  83.5 1.6 copy-done.5
  85.1 14.6 %cache_attention.1 = (bf16[1088,1024]{1,0:T(8,128)(2,1)S(1)}, f32[4,2,1088]{2,1,0:T(2,128)S(1)}) custom-call(s32[4]{0:T(128)S(1)} %reshape.213.range_ref, s32[1,128]{1,0:T(1,128)S(1)} %broadcast_in_dim_tile.6.lo_ref, s32[1,128]{1,0:T(1,128)S(1)} %broadcast_in_dim_tile.7.hi_ref, bf16[1088,1024]{1,0:T(8,128)(2,1)S(1)} %copy-done.2, ...), custom_call_target="tpu_custom_call" | custom-call | flops 4294967296 | bytes 8388608 | tf_op jit(solution)/shard_map/cache_attention/pallas_call | solution.py:122
  99.6 1.4 copy-done.3
  101.2 52.9 %all_gather.11 = f32[16,8,1088]{2,1,0:T(8,128)S(1)} all-gather(f32[1,8,1088]{2,1,0:T(8,128)S(1)} %all_gather_reshape.3), channel_id=1, replica_groups=mesh['seq'=16,'tp'=2] {'seq'}, dimensions={0}, use_global_device_ids=true | all-gather | bytes 591872 | tf_op jit(solution)/shard_map/all_gather | solution.py:262
  154.2 0.2 copy.25
  154.4 4.0 %mul.184 = f32[1088,8,128]{2,1,0:T(8,128)} broadcast(f32[1088,8]{1,0:T(8,128)S(1)} %copy.25), dimensions={0,1} | broadcast | bytes 4491264 | tf_op jit(solution)/shard_map/mul | solution.py:266
  158.5 5.1 %mul.185 = f32[16,68,1024]{2,1,0:T(8,128)} reshape(f32[1088,8,128]{2,1,0:T(8,128)} %mul.184) | data formatting | bytes 8912896 | tf_op jit(solution)/shard_map/mul | solution.py:266
  163.5 4.5 %reshape.215 = f32[16,68,1024]{2,1,0:T(8,128)} reshape(bf16[1088,1024]{1,0:T(8,128)(2,1)} %copy-done.3) | data formatting | bytes 6684672 | tf_op jit(solution)/shard_map/convert_element_type | solution.py:266
  168.1 6.1 %multiply_convert_fusion = bf16[16,68,1024]{2,1,0:T(8,128)(2,1)} fusion(f32[16,68,1024]{2,1,0:T(8,128)} %reshape.215, f32[16,68,1024]{2,1,0:T(8,128)} %mul.185), kind=kLoop, calls=%fused_computation | loop fusion | flops 2228224 | bytes 11141120 | tf_op jit(solution)/shard_map/convert_element_type | solution.py:267
  174.3 4.0 %reshape.218.k_ref.v_ref = bf16[1088,1024]{1,0:T(8,128)(2,1)} reshape(bf16[16,68,1024]{2,1,0:T(8,128)(2,1)} %all-gather.5.cloned.1.call-done) | data formatting | bytes 4456448
  178.3 1.6 copy-done.1
  180.0 5.5 %new_row_attention.1 = (f32[128,1024]{1,0:T(8,128)S(1)}, f32[4,2,128]{2,1,0:T(2,128)S(1)}) custom-call(s32[1,128]{1,0:T(1,128)S(1)} %get-tuple-element.25.lo_ref, s32[1,128]{1,0:T(1,128)S(1)} %get-tuple-element.26.hi_ref, bf16[128,1024]{1,0:T(8,128)(2,1)S(1)} %pad.4.q_ref, bf16[1088,1024]{1,0:T(8,128)(2,1)S(1)} %copy-done.1, bf16[1088,1024]{1,0:T(8,128)(2,1)S(1)} %copy-done.1), custom_call_target="tpu_custom_call" | custom-call | flops 570425344 | bytes 4194304 | tf_op jit(solution)/shard_map/new_row_attention/pallas_call | solution.py:175
  185.7 0.1 mul.181
  186.0 0.1 mul.187
  186.2 121.8 %reduce-scatter.3.cloned.1.call-done = bf16[1,68,1024]{2,1,0:T(8,128)(2,1)} async-done(((bf16[16,68,1024]{2,1,0:T(8,128)(2,1)}), bf16[1,68,1024]{2,1,0:T(8,128)(2,1)}) %reduce-scatter.3.cloned.1.call-update) | async-done | bytes 139280 | tf_op jit(solution)/shard_map/reduce_scatter | solution.py:268
  308.0 3.8 %convolution_convert_fusion = bf16[68,2048]{1,0:T(8,128)(2,1)} fusion(bf16[1024,2048]{1,0:T(8,128)(2,1)} %param.15, f32[68,1024]{1,0:T(8,128)S(1)} %bitcast.44, f32[68,1024]{1,0:T(8,128)S(1)} %bitcast.43, f32[128,1024]{1,0:T(8,128)S(1)} %get-tuple-element.9, bf16[1,68,1024]{2,1,0:T(8,128)(2,1)} %reduce-scatter.3.cloned.1.call-done), kind=kOutput, calls=%fused_computation.1 | convolution fusion | flops 285700096 | bytes 5496832 | tf_op jit(solution)/shard_map/dot_general | solution.py:293
  311.9 9.4 %reduce-scatter.5.cloned.1.call-done = bf16[68,1024]{1,0:T(8,128)(2,1)} async-done(((bf16[68,2048]{1,0:T(8,128)(2,1)}), bf16[68,1024]{1,0:T(8,128)(2,1)}) %reduce-scatter.5.cloned.1.call-update) | async-done | bytes 139280 | tf_op jit(solution)/shard_map/reduce_scatter | solution.py:294
  (59 shorter events, 2.0 us)
Async XLA Ops:
  6.5 7.4 %copy-start = (bf16[2048,512]{1,0:T(8,128)(2,1)S(1)}, bf16[2048,512]{1,0:T(8,128)(2,1)}, u32[]{:S(2)}) copy-start(bf16[2048,512]{1,0:T(8,128)(2,1)} %param.13) | copy-start | bytes 6291460
  6.5 69.7 %all-gather.7.cloned.1.call-start = ((), (), s32[]{:S(2)}) async-start(), calls=%async_computation.5 | async-start | bytes 2506752 | tf_op jit(solution)/shard_map/all_gather | solution.py:253
  12.5 1.4 copy-start.6
  13.9 160.4 %all-gather.5.cloned.1.call-start = ((), (), s32[]{:S(2)}) async-start(), calls=%async_computation.4 | async-start | bytes 2506752 | tf_op jit(solution)/shard_map/all_gather | solution.py:254
  14.5 4.0 %copy-start.7 = (s32[66]{0:T(128)S(1)}, s32[66]{0:T(128)}, u32[]{:S(2)}) copy-start(s32[66]{0:T(128)} %param.18) | copy-start | bytes 796
  17.8 290.2 %reduce-scatter.3.cloned.1.call-start = ((), (), s32[]{:S(2)}) async-start(), calls=%async_computation.2 | async-start | bytes 2506752 | tf_op jit(solution)/shard_map/reduce_scatter | solution.py:268
  80.3 1.6 copy-start.2
  81.9 1.6 copy-start.4
  83.5 1.6 copy-start.5
  99.6 1.5 copy-start.3
  174.2 147.1 %reduce-scatter.5.cloned.1.call-start = ((), (), s32[]{:S(2)}) async-start(), calls=%async_computation.3 | async-start | bytes 442368 | tf_op jit(solution)/shard_map/reduce_scatter | solution.py:294
  178.3 1.6 copy-start.1
Sparse Core Ops, SparseCore 0:
  14.0 62.1 all-gather.6
  79.1 63.4 all-gather.4
  174.3 133.6 reduce-scatter.2
  312.0 9.1 reduce-scatter.4

commit v2 on v1

--- a/solution.py
+++ b/solution.py
@@ -71,7 +71,6 @@
     groups = q_ref.shape[1] // HD
     boundary = PREFILLS * SPAN
     decodes = q_ref.shape[0] - boundary
-    tiles = k_ref.shape[0] // TILE
 
     def attend(q, lo, hi, first_tile, last_tile, width):
         begin(top_ref, sum_ref, acc_ref)
@@ -89,7 +88,17 @@
     q = jnp.concatenate(
         [q_ref[boundary:, g * HD:(g + 1) * HD] for g in range(groups)], axis=0
     )
-    out, lse = attend(q, lo_ref[...], hi_ref[...], 0, tiles, groups * decodes)
+    scores = nt_dot(k_ref[...], q) * SCALE
+    index = lax.broadcasted_iota(jnp.int32, scores.shape, 0)
+    visible = (index >= lo_ref[...]) & (index < hi_ref[...])
+    scores = jnp.where(visible, scores, NEGATIVE)
+    top = jnp.max(scores, axis=0, keepdims=True)
+    weights = jnp.where(visible, jnp.exp(scores - top), 0.0)
+    total = jnp.sum(weights, axis=0, keepdims=True)
+    some = total > 0.0
+    safe = jnp.where(some, total, 1.0)
+    out = tn_dot(v_ref[...], weights.astype(jnp.bfloat16)) / safe
+    lse = jnp.where(some, top + jnp.log(safe), NEGATIVE)
     out = out.T.astype(jnp.bfloat16)
     for g in range(groups):
         o_ref[boundary:, g * HD:(g + 1) * HD] = out[g * decodes:(g + 1) * decodes]
@@ -196,6 +205,149 @@
             flops=4 * count * q_width * rows, bytes_accessed=4 << 20, transcendentals=1 << 20
         ),
     )(lo, hi, queries, new, new)
+
+
+def flip(index, bit):
+    return index + bit - 2 * bit * ((index // bit) % 2)
+
+
+def greet(peers):
+    barrier = pltpu.get_barrier_semaphore()
+    for peer in peers:
+        pl.semaphore_signal(
+            barrier,
+            inc=1,
+            device_id=(peer, lax.axis_index("tp")),
+            device_id_type=pl.DeviceIdType.MESH,
+        )
+    pl.semaphore_wait(barrier, len(peers))
+
+
+def offset_index(index, offset, bits):
+    for bit in bits:
+        if offset & bit:
+            index = flip(index, bit)
+    return index
+
+
+def gather_kernel(bits, x_ref, out_ref, own_sem, send_sem, recv_sem):
+    me = lax.axis_index("seq")
+    greet([flip(me, bit) for bit in bits])
+    half = x_ref.shape[1] // 2
+    orders = [list(bits), list(bits[:-2]) + [bits[-1], bits[-2]]]
+    own = pltpu.make_async_copy(x_ref, out_ref.at[me], own_sem)
+    own.start()
+    held = [[0], [0]]
+    sends, got, number = [], {}, [0, 0]
+    for step in range(len(bits)):
+        fresh = [[], []]
+        for place in range(len(held[0])):
+            for part in range(2):
+                bit, offset = orders[part][step], held[part][place]
+                columns = pl.ds(part * half, half)
+                if offset and (part, offset) in got:
+                    got.pop((part, offset)).wait_recv()
+                block = offset_index(me, offset, bits)
+                copy = pltpu.make_async_remote_copy(
+                    src_ref=out_ref.at[block, :, columns] if offset else x_ref.at[:, columns],
+                    dst_ref=out_ref.at[block, :, columns],
+                    send_sem=send_sem.at[part, number[part]],
+                    recv_sem=recv_sem.at[part, offset ^ bit],
+                    device_id=(flip(me, bit), lax.axis_index("tp")),
+                    device_id_type=pl.DeviceIdType.MESH,
+                )
+                copy.start()
+                number[part] += 1
+                sends.append(copy)
+                fresh[part].append((offset ^ bit, copy))
+        for part in range(2):
+            for offset, copy in fresh[part]:
+                held[part].append(offset)
+                got[(part, offset)] = copy
+    for copy in got.values():
+        copy.wait_recv()
+    for copy in sends:
+        copy.wait_send()
+    own.wait()
+
+
+def gather(block, count):
+    bits = []
+    while 1 << len(bits) < count:
+        bits.insert(0, 1 << len(bits))
+    return pl.pallas_call(
+        functools.partial(gather_kernel, bits),
+        name="gather_rows",
+        out_shape=jax.ShapeDtypeStruct((count,) + block.shape, block.dtype),
+        in_specs=[pl.BlockSpec(memory_space=pl.ANY)],
+        out_specs=pl.BlockSpec(memory_space=pl.ANY),
+        scratch_shapes=[
+            pltpu.SemaphoreType.DMA,
+            pltpu.SemaphoreType.DMA((2, count - 1)),
+            pltpu.SemaphoreType.DMA((2, count)),
+        ],
+        compiler_params=pltpu.CompilerParams(collective_id=0, has_side_effects=True),
+        cost_estimate=pl.CostEstimate(
+            flops=0, bytes_accessed=100 << 20, transcendentals=0
+        ),
+    )(block)
+
+
+def exchange_kernel(count, x_ref, l_ref, out_ref, lout_ref, own_sem, send_sem, recv_sem):
+    me = lax.axis_index("seq")
+    peers = [lax.rem(me + k, count) for k in range(1, count)]
+    greet(peers)
+    own = pltpu.make_async_copy(x_ref.at[me], out_ref.at[me], own_sem.at[0])
+    own_lse = pltpu.make_async_copy(l_ref.at[me], lout_ref.at[me], own_sem.at[1])
+    own.start()
+    own_lse.start()
+    copies = []
+    for k in range(1, count):
+        for part, (source, target) in enumerate(((x_ref, out_ref), (l_ref, lout_ref))):
+            copy = pltpu.make_async_remote_copy(
+                src_ref=source.at[peers[k - 1]],
+                dst_ref=target.at[me],
+                send_sem=send_sem.at[part, k],
+                recv_sem=recv_sem.at[part, k],
+                device_id=(peers[k - 1], lax.axis_index("tp")),
+                device_id_type=pl.DeviceIdType.MESH,
+            )
+            copy.start()
+            copies.append((part, k, copy))
+    for part, k, copy in copies:
+        copy.wait_send()
+        copy.wait_recv()
+    own.wait()
+    own_lse.wait()
+
+
+def exchange(blocks, lse):
+    count = blocks.shape[0]
+    any_spec = pl.BlockSpec(memory_space=pl.ANY)
+    return pl.pallas_call(
+        functools.partial(exchange_kernel, count),
+        name="exchange_partials",
+        out_shape=(
+            jax.ShapeDtypeStruct(blocks.shape, blocks.dtype),
+            jax.ShapeDtypeStruct(lse.shape, lse.dtype),
+        ),
+        in_specs=[any_spec, any_spec],
+        out_specs=(any_spec, any_spec),
+        scratch_shapes=[
+            pltpu.SemaphoreType.DMA((2,)),
+            pltpu.SemaphoreType.DMA((2, count)),
+            pltpu.SemaphoreType.DMA((2, count)),
+        ],
+        compiler_params=pltpu.CompilerParams(collective_id=1, has_side_effects=True),
+        cost_estimate=pl.CostEstimate(
+            flops=0, bytes_accessed=160 << 20, transcendentals=0
+        ),
+    )(blocks, lse)
+
+
+def flat_blocks(values, count, flat):
+    values = values.reshape(count, -1, HD)
+    return jnp.pad(values, ((0, 0), (0, flat - values.shape[1]), (0, 0)))
 
 
 def per_device(
@@ -250,7 +402,12 @@
     )
     new_keys = rotate(new_keys, my_position).astype(jnp.bfloat16).reshape(tok_rows, kv_heads * HD)
     new_values = jnp.dot(normed, w_value, preferred_element_type=jnp.float32).astype(jnp.bfloat16)
-    gathered = lax.all_gather(queries, "seq", axis=0, tiled=True)
+    lines = tok_rows * q_heads
+    flat = -(-lines // 16) * 16
+    gathered = gather(
+        jnp.pad(queries, ((0, -(-tok_rows // 16) * 16 - tok_rows), (0, 0))), seq_count
+    )
+    gathered = gathered[:, :tok_rows].reshape(all_rows, q_heads * HD)
     new = lax.all_gather(
         jnp.concatenate([new_keys, new_values], axis=1), "seq", axis=0, tiled=True
     )
@@ -258,14 +415,15 @@
     part, part_lse = cache_attention(
         ranges, decode_lo, decode_hi, gathered, cache_keys, cache_values
     )
-    part_lse = part_lse.reshape(q_heads, all_rows)
-    every_lse = lax.all_gather(part_lse, "seq", axis=0)
-    most = jnp.max(every_lse, axis=0)
-    cache_lse = most + jnp.log(jnp.sum(jnp.exp(every_lse - most[None]), axis=0))
-    share = jnp.where(part_lse > 0.5 * NEGATIVE, jnp.exp(part_lse - cache_lse), 0.0)
-    part = part.reshape(all_rows, q_heads, HD).astype(jnp.float32) * share.T[:, :, None]
-    part = part.astype(jnp.bfloat16).reshape(seq_count, tok_rows, q_heads * HD)
-    cached = lax.psum_scatter(part, "seq", scatter_dimension=0)
+    part_lse = part_lse.reshape(q_heads, seq_count, tok_rows).transpose(1, 0, 2)
+    lanes = -(-tok_rows // 128) * 128
+    head_rows = -(-q_heads // 8) * 8
+    part_lse = jnp.pad(
+        part_lse, ((0, 0), (0, head_rows - q_heads), (0, lanes - tok_rows))
+    )
+    parts, parts_lse = exchange(flat_blocks(part, seq_count, flat), part_lse)
+    parts = parts[:, :lines].reshape(seq_count, tok_rows, q_heads, HD)
+    parts_lse = parts_lse[:, :q_heads, :tok_rows].transpose(0, 2, 1)
 
     padded = -(-tok_rows // 128) * 128
     lane_rows = seq_index * tok_rows + jnp.minimum(
@@ -279,16 +437,14 @@
         new,
     )
     own = own[:tok_rows].reshape(tok_rows, q_heads, HD)
-    own_lse = own_lse.reshape(q_heads, padded)[:, :tok_rows]
-    my_cache_lse = lax.dynamic_slice_in_dim(cache_lse, seq_index * tok_rows, tok_rows, axis=1)
-    top = jnp.maximum(own_lse, my_cache_lse)
+    own_lse = own_lse.reshape(q_heads, padded)[:, :tok_rows].T
+    top = jnp.maximum(own_lse, jnp.max(parts_lse, axis=0))
     own_weight = jnp.exp(own_lse - top)
-    cache_weight = jnp.exp(my_cache_lse - top)
-    norm = own_weight + cache_weight
-    own_weight = (own_weight / norm).T[:, :, None]
-    cache_weight = (cache_weight / norm).T[:, :, None]
-    cached = cached.reshape(tok_rows, q_heads, HD).astype(jnp.float32)
-    attended = (own * own_weight + cached * cache_weight).astype(jnp.bfloat16)
+    weights = jnp.exp(parts_lse - top[None])
+    norm = own_weight + jnp.sum(weights, axis=0)
+    cached = jnp.sum(parts.astype(jnp.float32) * weights[..., None], axis=0)
+    attended = (own * own_weight[..., None] + cached) / norm[..., None]
+    attended = attended.astype(jnp.bfloat16)
     attended = attended.reshape(tok_rows, q_heads * HD)
     partial_out = jnp.dot(attended, w_out, preferred_element_type=jnp.float32)
     return lax.psum_scatter(partial_out.astype(jnp.bfloat16), "tp", scatter_dimension=1, tiled=True)

time: 325 us -> 196 us (0.60); the launches traced: 328 us -> 195 us
  waiting for transfers between devices: 188 us -> 9.78 us
  Pallas kernels: 20 us -> 122 us
  blocking collectives: 52.9 us -> 0 us
    reduce_scatter x1 -> x0, waiting for transfers between devices: 122 us -> none  [per_device(): cached = lax.psum_scatter(part, 'seq', scatter_dimension=0)]
    pallas_call x0 -> x2, Pallas kernels: none -> 109 us  [the longest x1 70.9 us: exchange(): pl.pallas_call(functools.partial(exchange_kernel, count), name='exchange_...]
    all_gather x1 -> x0, waiting for transfers between devices: 57.1 us -> none  [per_device(): gathered = lax.all_gather(queries, 'seq', axis=0, tiled=True)]
    all_gather x1 -> x0, blocking collectives: 52.9 us -> none  [per_device(): every_lse = lax.all_gather(part_lse, 'seq', axis=0)]
    reshape x1 -> x4, local copies, waits for them, and re-layouts: 0.03 us -> 8.85 us  [the longest x1 4.71 us: flat_blocks(): values = values.reshape(count, -1, HD)]
    mul x4 -> x2, local copies, waits for them, and re-layouts: 9.36 us -> 1.19 us  [the longest x1 1.07 us: per_device(): cached = jnp.sum(parts.astype(jnp.float32) * weights[..., None], axis=0)]
    pallas_call x1, Pallas kernels: 14.6 us -> 7.35 us  [cache_attention(): pl.pallas_call(cache_kernel, name='cache_attention', grid=(kv_heads,), ou...]
    convert_element_type x1 -> x0, other arithmetic: 6.07 us -> none  [per_device(): part = part.astype(jnp.bfloat16).reshape(seq_count, tok_rows, q_heads * HD)]
  transfers between devices with their start and end apart: 4 -> 2, of which waited for: 3 -> 1; matrix products, arithmetic and copies ran while one was open for 10% -> 10% of each run, Pallas kernels for 6% -> 60%
where the time goes in v2:
time: 196 us; the launch traced here: 195 us
  Pallas kernels  122 us (62%)
  local copies, waits for them, and re-layouts  30.4 us (16%)
  between operations  14.4 us (7%)
  waiting for transfers between devices  9.78 us (5%)
  other arithmetic  9.35 us (5%)
  matrix products  8.96 us (5%)
    pallas_call x1, Pallas kernels, exchange(): pl.pallas_call(functools.partial(exchange_kernel, count), name='exchange_...  70.9 us
    pallas_call x1, Pallas kernels, gather(): pl.pallas_call(functools.partial(gather_kernel, bits), name='gather_rows'...  38.5 us
    unnamed x30, local copies, waits for them, and re-layouts  12.2 us
    reduce_scatter x1, waiting for transfers between devices, per_device(): lax.psum_scatter(partial_out.astype(jnp.bfloat16), 'tp', scatter_dimensio...  9.73 us
    pallas_call x1, Pallas kernels, cache_attention(): pl.pallas_call(cache_kernel, name='cache_attention', grid=(kv_heads,), ou...  7.35 us
    pallas_call x1, Pallas kernels, self_attention(): pl.pallas_call(self_kernel, name='new_row_attention', grid=(kv_heads,), o...  5.49 us
    reshape x1, local copies, waits for them, and re-layouts, flat_blocks(): values = values.reshape(count, -1, HD)  4.71 us
    reshape x1, local copies, waits for them, and re-layouts, per_device(): gathered = gathered[:, :tok_rows].reshape(all_rows, q_heads * HD)  4.01 us
  transfers between devices with their start and end apart: 2, of which 1 were waited for; matrix products, arithmetic and copies ran while one was open for 10% of the time, Pallas kernels for 60%

profile of v2, /device:TPU:15, one launch (start us, length us, event | category | flops | bytes accessed | tf_op | source)
XLA Modules:
  0.0 195.1 jit_solution(4181208036707487343)
XLA Ops:
  6.6 1.3 fusion
  7.9 0.9 select_reduce_fusion.1
  8.8 0.7 convert_element_type.48
  9.5 1.5 convolution_convert_fusion.1
  11.0 0.5 fusion.8
  11.6 0.2 multiply_cosine_fusion
  11.8 0.2 subtract_convert_fusion.1
  12.2 0.7 maximum_bitcast_fusion
  12.9 3.1 %fusion.10 = f32[68,1024]{1,0:T(8,128)S(1)} fusion(bf16[2048,1024]{1,0:T(8,128)(2,1)} %param.12, bf16[68,2048]{1,0:T(8,128)(2,1)S(1)} %copy-done.6, f32[2048]{0:T(1024)S(1)} %convert_element_type.48, f32[68]{0:T(128)S(1)} %add_rsqrt_fusion), kind=kOutput, calls=%fused_computation.53 | convolution fusion | flops 285769728 | bytes 4759824 | tf_op jit(solution)/shard_map/dot_general | solution.py:396
  16.1 0.2 subtract_convert_fusion
  16.5 0.7 pad.13.x_ref
  18.5 38.5 %gather_rows.1 = bf16[16,80,1024]{2,1,0:T(8,128)(2,1)} custom-call(bf16[80,1024]{1,0:T(8,128)(2,1)} %pad.13.x_ref), custom_call_target="tpu_custom_call" | custom-call | bytes 104857600 | tf_op jit(solution)/shard_map/gather_rows/pallas_call | solution.py:278
  57.0 3.3 %slice.46 = bf16[16,68,1024]{2,1,0:T(8,128)(2,1)} slice(bf16[16,80,1024]{2,1,0:T(8,128)(2,1)} %gather_rows.1), slice={[0:16], [0:68], [0:1024]} | slice | bytes 4456448 | tf_op jit(solution)/shard_map/slice | solution.py:410
  60.4 4.0 %reshape.217.q_ref = bf16[1088,1024]{1,0:T(8,128)(2,1)} reshape(bf16[16,68,1024]{2,1,0:T(8,128)(2,1)} %slice.46) | data formatting | bytes 4456448 | tf_op jit(solution)/shard_map/reshape | solution.py:410
  64.4 1.6 copy-done.2
  66.0 1.6 copy-done.4
  67.6 1.6 copy-done.5
  69.2 7.3 %cache_attention.1 = (bf16[1088,1024]{1,0:T(8,128)(2,1)S(1)}, f32[4,2,1088]{2,1,0:T(2,128)S(1)}) custom-call(s32[4]{0:T(128)S(1)} %reshape.216.range_ref, s32[1,128]{1,0:T(1,128)S(1)} %broadcast_in_dim_tile.6.lo_ref, s32[1,128]{1,0:T(1,128)S(1)} %broadcast_in_dim_tile.7.hi_ref, bf16[1088,1024]{1,0:T(8,128)(2,1)S(1)} %copy-done.2, ...), custom_call_target="tpu_custom_call" | custom-call | flops 4294967296 | bytes 8388608 | tf_op jit(solution)/shard_map/cache_attention/pallas_call | solution.py:131
  76.5 1.4 copy-done.3
  77.9 4.7 %reshape.218.x_ref = bf16[16,544,128]{2,1,0:T(8,128)(2,1)} reshape(bf16[1088,1024]{1,0:T(8,128)(2,1)} %copy-done.3) | data formatting | bytes 4456448 | tf_op jit(solution)/shard_map/reshape | solution.py:349
  82.8 0.6 pad.14.l_ref
  83.4 70.9 %exchange_partials.1 = (bf16[16,544,128]{2,1,0:T(8,128)(2,1)}, f32[16,8,128]{2,1,0:T(8,128)}) custom-call(bf16[16,544,128]{2,1,0:T(8,128)(2,1)} %reshape.218.x_ref, f32[16,8,128]{2,1,0:T(8,128)} %pad.14.l_ref), custom_call_target="tpu_custom_call" | custom-call | bytes 167772160 | tf_op jit(solution)/shard_map/exchange_partials/pallas_call | solution.py:327
  154.3 0.9 bitcast_reduce_fusion
  155.2 4.0 %reshape.221.k_ref.v_ref = bf16[1088,1024]{1,0:T(8,128)(2,1)} reshape(bf16[16,68,1024]{2,1,0:T(8,128)(2,1)} %all-gather.3.cloned.1.call-done) | data formatting | bytes 4456448
  159.2 1.6 copy-done.1
  160.9 5.5 %new_row_attention.1 = (f32[128,1024]{1,0:T(8,128)S(1)}, f32[4,2,128]{2,1,0:T(2,128)S(1)}) custom-call(s32[1,128]{1,0:T(1,128)S(1)} %get-tuple-element.31.lo_ref, s32[1,128]{1,0:T(1,128)S(1)} %get-tuple-element.32.hi_ref, bf16[128,1024]{1,0:T(8,128)(2,1)S(1)} %pad.12.q_ref, bf16[1088,1024]{1,0:T(8,128)(2,1)S(1)} %copy-done.1, bf16[1088,1024]{1,0:T(8,128)(2,1)S(1)} %copy-done.1), custom_call_target="tpu_custom_call" | custom-call | flops 570425344 | bytes 4194304 | tf_op jit(solution)/shard_map/new_row_attention/pallas_call | solution.py:184
  167.1 0.9 copy.29
  168.0 1.1 copy.30
  169.0 3.9 %multiply_reduce_fusion = f32[544,128]{1,0:T(8,128)} fusion(bf16[16,544,128]{2,1,0:T(8,128)(2,1)} %get-tuple-element.16, f32[16,544]{1,0:T(8,128)S(1)} %copy.30), kind=kLoop, calls=%fused_computation | loop fusion | flops 3272704 | bytes 2541568 | tf_op jit(solution)/shard_map/reduce_sum | solution.py:445
  173.0 1.7 reduce_sum.51
  174.7 3.8 %convolution_convert_fusion = bf16[68,2048]{1,0:T(8,128)(2,1)} fusion(bf16[1024,2048]{1,0:T(8,128)(2,1)} %param.15, f32[68,1024]{1,0:T(8,128)S(1)} %bitcast.48, f32[68,1024]{1,0:T(8,128)} %reduce_sum.51, f32[68,1024]{1,0:T(8,128)S(1)} %bitcast.47, f32[128,1024]{1,0:T(8,128)S(1)} %get-tuple-element.11), kind=kOutput, calls=%fused_computation.1 | convolution fusion | flops 285630464 | bytes 5636096 | tf_op jit(solution)/shard_map/dot_general | solution.py:449
  178.5 9.7 %reduce-scatter.2.cloned.1.call-done = bf16[68,1024]{1,0:T(8,128)(2,1)} async-done(((bf16[68,2048]{1,0:T(8,128)(2,1)}), bf16[68,1024]{1,0:T(8,128)(2,1)}) %reduce-scatter.2.cloned.1.call-update) | async-done | bytes 139280 | tf_op jit(solution)/shard_map/reduce_scatter | solution.py:450
  (60 shorter events, 2.0 us)
Async XLA Ops:
  6.5 2.9 %copy-start = (bf16[2048,512]{1,0:T(8,128)(2,1)S(1)}, bf16[2048,512]{1,0:T(8,128)(2,1)}, u32[]{:S(2)}) copy-start(bf16[2048,512]{1,0:T(8,128)(2,1)} %param.14) | copy-start | bytes 6291460
  6.5 4.4 %copy-start.6 = (bf16[68,2048]{1,0:T(8,128)(2,1)S(1)}, bf16[68,2048]{1,0:T(8,128)(2,1)}, u32[]{:S(2)}) copy-start(bf16[68,2048]{1,0:T(8,128)(2,1)} %param.10) | copy-start | bytes 835588
  6.5 148.6 %all-gather.3.cloned.1.call-start = ((), (), s32[]{:S(2)}) async-start(), calls=%async_computation.2 | async-start | bytes 2506752 | tf_op jit(solution)/shard_map/all_gather | solution.py:411
  7.9 3.1 %copy-start.7 = (bf16[2048,512]{1,0:T(8,128)(2,1)S(1)}, bf16[2048,512]{1,0:T(8,128)(2,1)}, u32[]{:S(2)}) copy-start(bf16[2048,512]{1,0:T(8,128)(2,1)} %param.13) | copy-start | bytes 6291460
  12.9 175.4 %reduce-scatter.2.cloned.1.call-start = ((), (), s32[]{:S(2)}) async-start(), calls=%async_computation.1 | async-start | bytes 442368 | tf_op jit(solution)/shard_map/reduce_scatter | solution.py:450
  16.0 1.8 copy-start.9
  64.4 1.6 copy-start.2
  66.0 1.6 copy-start.4
  67.6 1.6 copy-start.5
  76.5 1.4 copy-start.3
  159.2 1.6 copy-start.1
  160.9 5.5 %copy-start.8 = (f32[16,8,128]{2,1,0:T(8,128)S(1)}, f32[16,8,128]{2,1,0:T(8,128)}, u32[]{:S(2)}) copy-start(f32[16,8,128]{2,1,0:T(8,128)} %get-tuple-element.15) | copy-start | bytes 196612
Sparse Core Ops, SparseCore 0:
  13.0 67.3 all-gather.2
  178.7 9.5 reduce-scatter.1

commit v3 on v2

--- a/solution.py
+++ b/solution.py
@@ -67,10 +67,19 @@
     return out, jnp.where(some, top_ref[:, :width] + jnp.log(safe), NEGATIVE)
 
 
-def cache_kernel(range_ref, lo_ref, hi_ref, q_ref, k_ref, v_ref, o_ref, l_ref, top_ref, sum_ref, acc_ref):
+def unpack(source, target):
+    rows = target.shape[0] // source.shape[0]
+    for block in range(source.shape[0]):
+        target[block * rows:(block + 1) * rows, :] = source[block, :rows, :].astype(jnp.float32)
+
+
+def cache_kernel(
+    range_ref, lo_ref, hi_ref, blocks_ref, k_ref, v_ref, o_ref, l_ref, top_ref, sum_ref, acc_ref, q_ref
+):
     groups = q_ref.shape[1] // HD
     boundary = PREFILLS * SPAN
     decodes = q_ref.shape[0] - boundary
+    unpack(blocks_ref, q_ref)
 
     def attend(q, lo, hi, first_tile, last_tile, width):
         begin(top_ref, sum_ref, acc_ref)
@@ -87,7 +96,7 @@
 
     q = jnp.concatenate(
         [q_ref[boundary:, g * HD:(g + 1) * HD] for g in range(groups)], axis=0
-    )
+    ).astype(jnp.bfloat16)
     scores = nt_dot(k_ref[...], q) * SCALE
     index = lax.broadcasted_iota(jnp.int32, scores.shape, 0)
     visible = (index >= lo_ref[...]) & (index < hi_ref[...])
@@ -110,7 +119,7 @@
         @pl.when(hi > lo)
         def _():
             for g in range(groups):
-                q = q_ref[rows, g * HD:(g + 1) * HD]
+                q = q_ref[rows, g * HD:(g + 1) * HD].astype(jnp.bfloat16)
                 out, lse = attend(q, lo, hi, lo // TILE, (hi + TILE - 1) // TILE, SPAN)
                 o_ref[rows, g * HD:(g + 1) * HD] = out.T.astype(jnp.bfloat16)
                 l_ref[0, g:g + 1, rows] = lse
@@ -121,8 +130,8 @@
             l_ref[0, :, rows] = jnp.full((groups, SPAN), NEGATIVE, jnp.float32)
 
 
-def cache_attention(ranges, lo, hi, queries, keys, values):
-    rows, q_width = queries.shape
+def cache_attention(rows, ranges, lo, hi, queries, keys, values):
+    count, padded, q_width = queries.shape
     slots, kv_width = keys.shape
     kv_heads = kv_width // HD
     groups = q_width // kv_width
@@ -140,7 +149,7 @@
             pl.BlockSpec(memory_space=pltpu.SMEM),
             pl.BlockSpec(lo.shape, whole),
             pl.BlockSpec(hi.shape, whole),
-            pl.BlockSpec((rows, groups * HD), column),
+            pl.BlockSpec((count, padded, groups * HD), lambda c: (0, 0, c)),
             pl.BlockSpec((slots, HD), column),
             pl.BlockSpec((slots, HD), column),
         ],
@@ -152,6 +161,7 @@
             pltpu.VMEM((1, SPAN), jnp.float32),
             pltpu.VMEM((1, SPAN), jnp.float32),
             pltpu.VMEM((HD, SPAN), jnp.float32),
+            pltpu.VMEM((rows, groups * HD), jnp.float32),
         ],
         compiler_params=pltpu.CompilerParams(vmem_limit_bytes=32 << 20),
         cost_estimate=pl.CostEstimate(
@@ -160,9 +170,12 @@
     )(ranges, lo, hi, queries, keys, values)
 
 
-def self_kernel(lo_ref, hi_ref, q_ref, k_ref, v_ref, o_ref, l_ref):
+def self_kernel(lo_ref, hi_ref, q_ref, k_ref, v_ref, o_ref, l_ref, keys_ref, values_ref):
     groups = q_ref.shape[1] // HD
-    keys, values = k_ref[...], v_ref[...]
+    unpack(k_ref, keys_ref)
+    unpack(v_ref, values_ref)
+    keys = keys_ref[...].astype(jnp.bfloat16)
+    values = values_ref[...].astype(jnp.bfloat16)
     for g in range(groups):
         scores = nt_dot(keys, q_ref[:, g * HD:(g + 1) * HD]) * SCALE
         index = lax.broadcasted_iota(jnp.int32, scores.shape, 0)
@@ -178,7 +191,8 @@
 
 def self_attention(lo, hi, queries, new):
     rows, q_width = queries.shape
-    count, width = new.shape
+    blocks, block_rows, width = new.shape
+    count = blocks * block_rows
     kv_heads = width // (2 * HD)
     groups = q_width // HD // kv_heads
     return pl.pallas_call(
@@ -193,13 +207,14 @@
             pl.BlockSpec(lo.shape, lambda c: (0, 0)),
             pl.BlockSpec(hi.shape, lambda c: (0, 0)),
             pl.BlockSpec((rows, groups * HD), lambda c: (0, c)),
-            pl.BlockSpec((count, HD), lambda c: (0, c)),
-            pl.BlockSpec((count, HD), lambda c: (0, kv_heads + c)),
+            pl.BlockSpec((blocks, block_rows, HD), lambda c: (0, 0, c)),
+            pl.BlockSpec((blocks, block_rows, HD), lambda c: (0, 0, kv_heads + c)),
         ],
         out_specs=(
             pl.BlockSpec((rows, groups * HD), lambda c: (0, c)),
             pl.BlockSpec((1, groups, rows), lambda c: (c, 0, 0)),
         ),
+        scratch_shapes=[pltpu.VMEM((count, HD), jnp.float32)] * 2,
         compiler_params=pltpu.CompilerParams(vmem_limit_bytes=32 << 20),
         cost_estimate=pl.CostEstimate(
             flops=4 * count * q_width * rows, bytes_accessed=4 << 20, transcendentals=1 << 20
@@ -345,6 +360,74 @@
     )(blocks, lse)
 
 
+def project_kernel(count, a_ref, w_ref, o_ref, send_ref, recv_ref, send_sem, recv_sem):
+    me = lax.axis_index("tp")
+    columns = o_ref.shape[1]
+    peers = [lax.rem(me + k, count) for k in range(1, count)]
+    barrier = pltpu.get_barrier_semaphore()
+    for peer in peers:
+        pl.semaphore_signal(
+            barrier,
+            inc=1,
+            device_id=(lax.axis_index("seq"), peer),
+            device_id_type=pl.DeviceIdType.MESH,
+        )
+    def product(owner):
+        return jnp.dot(
+            a_ref[...],
+            w_ref[:, pl.ds(pl.multiple_of(owner * columns, columns), columns)],
+            preferred_element_type=jnp.float32,
+        )
+
+    copies = []
+    for k in range(1, count):
+        send_ref[k - 1] = product(peers[k - 1]).astype(jnp.bfloat16)
+        if k == 1:
+            pl.semaphore_wait(barrier, count - 1)
+        copy = pltpu.make_async_remote_copy(
+            src_ref=send_ref.at[k - 1],
+            dst_ref=recv_ref.at[k - 1],
+            send_sem=send_sem.at[k - 1],
+            recv_sem=recv_sem.at[k - 1],
+            device_id=(lax.axis_index("seq"), peers[k - 1]),
+            device_id_type=pl.DeviceIdType.MESH,
+        )
+        copy.start()
+        copies.append(copy)
+    total = product(me)
+    for k, copy in enumerate(copies):
+        copy.wait_recv()
+        total = total + recv_ref[k].astype(jnp.float32)
+    o_ref[...] = total.astype(jnp.bfloat16)
+    for copy in copies:
+        copy.wait_send()
+
+
+def project(attended, w_out, count):
+    rows = attended.shape[0]
+    columns = w_out.shape[1] // count
+    vmem = pl.BlockSpec(memory_space=pltpu.VMEM)
+    return pl.pallas_call(
+        functools.partial(project_kernel, count),
+        name="project_and_add",
+        out_shape=jax.ShapeDtypeStruct((rows, columns), jnp.bfloat16),
+        in_specs=[vmem, vmem],
+        out_specs=vmem,
+        scratch_shapes=[
+            pltpu.VMEM((count - 1, rows, columns), jnp.bfloat16),
+            pltpu.VMEM((count - 1, rows, columns), jnp.bfloat16),
+            pltpu.SemaphoreType.DMA((count - 1,)),
+            pltpu.SemaphoreType.DMA((count - 1,)),
+        ],
+        compiler_params=pltpu.CompilerParams(
+            collective_id=2, has_side_effects=True, vmem_limit_bytes=24 << 20
+        ),
+        cost_estimate=pl.CostEstimate(
+            flops=2 * rows * w_out.size, bytes_accessed=8 << 20, transcendentals=0
+        ),
+    )(attended, w_out)
+
+
 def flat_blocks(values, count, flat):
     values = values.reshape(count, -1, HD)
     return jnp.pad(values, ((0, 0), (0, flat - values.shape[1]), (0, 0)))
@@ -407,13 +490,10 @@
     gathered = gather(
         jnp.pad(queries, ((0, -(-tok_rows // 16) * 16 - tok_rows), (0, 0))), seq_count
     )
-    gathered = gathered[:, :tok_rows].reshape(all_rows, q_heads * HD)
-    new = lax.all_gather(
-        jnp.concatenate([new_keys, new_values], axis=1), "seq", axis=0, tiled=True
-    )
+    new = lax.all_gather(jnp.concatenate([new_keys, new_values], axis=1), "seq", axis=0)
 
     part, part_lse = cache_attention(
-        ranges, decode_lo, decode_hi, gathered, cache_keys, cache_values
+        all_rows, ranges, decode_lo, decode_hi, gathered, cache_keys, cache_values
     )
     part_lse = part_lse.reshape(q_heads, seq_count, tok_rows).transpose(1, 0, 2)
     lanes = -(-tok_rows // 128) * 128
@@ -446,8 +526,8 @@
     attended = (own * own_weight[..., None] + cached) / norm[..., None]
     attended = attended.astype(jnp.bfloat16)
     attended = attended.reshape(tok_rows, q_heads * HD)
-    partial_out = jnp.dot(attended, w_out, preferred_element_type=jnp.float32)
-    return lax.psum_scatter(partial_out.astype(jnp.bfloat16), "tp", scatter_dimension=1, tiled=True)
+    attended = jnp.pad(attended, ((0, -(-tok_rows // 16) * 16 - tok_rows), (0, 0)))
+    return project(attended, w_out, lax.axis_size("tp"))[:tok_rows]
 
 
 def solution(mesh):

time: 196 us -> 177 us (0.903); the launches traced: 195 us -> 180 us
  waiting for transfers between devices: 9.78 us -> 0.03 us
  local copies, waits for them, and re-layouts: 30.4 us -> 21.9 us
  Pallas kernels: 122 us -> 128 us
  matrix products: 8.96 us -> 5.12 us
    reduce_scatter x1 -> x0, waiting for transfers between devices: 9.73 us -> none  [per_device(): lax.psum_scatter(partial_out.astype(jnp.bfloat16), 'tp', scatter_dimensio...]
    reshape x1 -> x0, local copies, waits for them, and re-layouts: 4.01 us -> none  [per_device(): gathered = gathered[:, :tok_rows].reshape(all_rows, q_heads * HD)]
    dot_general x1 -> x0, matrix products: 3.84 us -> none  [per_device(): partial_out = jnp.dot(attended, w_out, preferred_element_type=jnp.float32)]
    pallas_call x0 -> x1, Pallas kernels: none -> 3.33 us  [project(): pl.pallas_call(functools.partial(project_kernel, count), name='project_an...]
    slice x1, local copies, waits for them, and re-layouts: 3.35 us -> 0.67 us  [per_device(): return project(attended, w_out, lax.axis_size('tp'))[:tok_rows]]
    pallas_call x1, Pallas kernels: 70.9 us -> 73.2 us  [exchange(): pl.pallas_call(functools.partial(exchange_kernel, count), name='exchange_...]
    unnamed x30 -> x31, local copies, waits for them, and re-layouts: 12.2 us -> 10.4 us
  transfers between devices with their start and end apart: 2 -> 1, of which waited for: 1 -> 0; matrix products, arithmetic and copies ran while one was open for 10% -> 6% of each run, Pallas kernels for 60% -> 66%
where the time goes in v3:
time: 177 us; the launch traced here: 180 us
  Pallas kernels  128 us (72%)
  local copies, waits for them, and re-layouts  21.9 us (12%)
  between operations  14.4 us (8%)
  other arithmetic  10.4 us (6%)
  matrix products  5.12 us (3%)
    pallas_call x1, Pallas kernels, exchange(): pl.pallas_call(functools.partial(exchange_kernel, count), name='exchange_...  73.2 us
    pallas_call x1, Pallas kernels, gather(): pl.pallas_call(functools.partial(gather_kernel, bits), name='gather_rows'...  38.5 us
    unnamed x31, local copies, waits for them, and re-layouts  10.4 us
    pallas_call x1, Pallas kernels, cache_attention(): pl.pallas_call(cache_kernel, name='cache_attention', grid=(kv_heads,), ou...  7.67 us
    pallas_call x1, Pallas kernels, self_attention(): pl.pallas_call(self_kernel, name='new_row_attention', grid=(kv_heads,), o...  5.76 us
    reshape x1, local copies, waits for them, and re-layouts, flat_blocks(): values = values.reshape(count, -1, HD)  4.68 us
    reduce_sum x1, other arithmetic, per_device(): cached = jnp.sum(parts.astype(jnp.float32) * weights[..., None], axis=0)  3.93 us
  transfers between devices with their start and end apart: 1, of which 0 were waited for; matrix products, arithmetic and copies ran while one was open for 6% of the time, Pallas kernels for 66%

profile of v3, /device:TPU:15, one launch (start us, length us, event | category | flops | bytes accessed | tf_op | source)
XLA Modules:
  0.0 180.3 jit_solution(17011241214089879825)
XLA Ops:
  6.6 1.3 fusion
  7.9 0.9 select_reduce_fusion.1
  8.8 0.7 convert_element_type.46
  9.5 1.5 convolution_convert_fusion
  11.0 0.5 fusion.8
  11.6 0.2 multiply_cosine_fusion
  11.8 0.2 subtract_convert_fusion.1
  12.2 0.7 maximum_bitcast_fusion
  12.9 3.1 %fusion.10 = f32[68,1024]{1,0:T(8,128)S(1)} fusion(bf16[2048,1024]{1,0:T(8,128)(2,1)} %param.12, bf16[68,2048]{1,0:T(8,128)(2,1)S(1)} %copy-done.7, f32[2048]{0:T(1024)S(1)} %convert_element_type.46, f32[68]{0:T(128)S(1)} %add_rsqrt_fusion), kind=kOutput, calls=%fused_computation.52 | convolution fusion | flops 285769728 | bytes 4759824 | tf_op jit(solution)/shard_map/dot_general | solution.py:479
  16.1 0.2 subtract_convert_fusion
  16.4 0.7 pad.16.x_ref
  18.4 38.5 %gather_rows.1.blocks_ref = bf16[16,80,1024]{2,1,0:T(8,128)(2,1)} custom-call(bf16[80,1024]{1,0:T(8,128)(2,1)} %pad.16.x_ref), custom_call_target="tpu_custom_call" | custom-call | bytes 104857600 | tf_op jit(solution)/shard_map/gather_rows/pallas_call | solution.py:293
  57.0 1.7 copy-done.3
  58.7 1.6 copy-done.5
  60.3 1.6 copy-done.6
  61.9 7.7 %cache_attention.1 = (bf16[1088,1024]{1,0:T(8,128)(2,1)S(1)}, f32[4,2,1088]{2,1,0:T(2,128)S(1)}) custom-call(s32[4]{0:T(128)S(1)} %reshape.213.range_ref, s32[1,128]{1,0:T(1,128)S(1)} %broadcast_in_dim_tile.6.lo_ref, s32[1,128]{1,0:T(1,128)S(1)} %broadcast_in_dim_tile.7.hi_ref, bf16[16,80,1024]{2,1,0:T(8,128)(2,1)S(1)} %copy-done.3, ...), custom_call_target="tpu_custom_call" | custom-call | flops 4294967296 | bytes 8388608 | tf_op jit(solution)/shard_map/cache_attention/pallas_call | solution.py:140
  69.6 1.3 copy-done.4
  70.9 4.7 %reshape.214.x_ref = bf16[16,544,128]{2,1,0:T(8,128)(2,1)} reshape(bf16[1088,1024]{1,0:T(8,128)(2,1)} %copy-done.4) | data formatting | bytes 4456448 | tf_op jit(solution)/shard_map/reshape | solution.py:432
  75.8 0.6 pad.17.l_ref
  76.4 73.2 %exchange_partials.1 = (bf16[16,544,128]{2,1,0:T(8,128)(2,1)}, f32[16,8,128]{2,1,0:T(8,128)}) custom-call(bf16[16,544,128]{2,1,0:T(8,128)(2,1)} %reshape.214.x_ref, f32[16,8,128]{2,1,0:T(8,128)} %pad.17.l_ref), custom_call_target="tpu_custom_call" | custom-call | bytes 167772160 | tf_op jit(solution)/shard_map/exchange_partials/pallas_call | solution.py:342
  149.6 0.9 bitcast_reduce_fusion
  150.5 1.7 copy-done.1
  152.2 5.8 %new_row_attention.1 = (f32[128,1024]{1,0:T(8,128)S(1)}, f32[4,2,128]{2,1,0:T(2,128)S(1)}) custom-call(s32[1,128]{1,0:T(1,128)S(1)} %get-tuple-element.31.lo_ref, s32[1,128]{1,0:T(1,128)S(1)} %get-tuple-element.32.hi_ref, bf16[128,1024]{1,0:T(8,128)(2,1)S(1)} %pad.15.q_ref, bf16[16,68,1024]{2,1,0:T(8,128)(2,1)S(1)} %copy-done.1, ...), custom_call_target="tpu_custom_call" | custom-call | flops 570425344 | bytes 4194304 | tf_op jit(solution)/shard_map/new_row_attention/pallas_call | solution.py:198
  158.2 0.1 mul.169
  158.6 0.9 copy.29
  159.5 1.1 copy.30
  160.6 3.9 %multiply_reduce_fusion = f32[544,128]{1,0:T(8,128)} fusion(bf16[16,544,128]{2,1,0:T(8,128)(2,1)} %get-tuple-element.16, f32[16,544]{1,0:T(8,128)S(1)} %copy.30), kind=kLoop, calls=%fused_computation | loop fusion | flops 3272704 | bytes 2541568 | tf_op jit(solution)/shard_map/reduce_sum | solution.py:525
  164.5 1.7 reduce_sum.51
  166.2 1.0 divide_convert_fusion
  167.3 2.2 %copy-done.2 = bf16[1024,2048]{1,0:T(8,128)(2,1)S(1)} copy-done((bf16[1024,2048]{1,0:T(8,128)(2,1)S(1)}, bf16[1024,2048]{1,0:T(8,128)(2,1)}, u32[]{:S(2)}) %copy-start.2) | copy-done | bytes 4194328
  169.5 3.3 %project_and_add.1 = bf16[80,1024]{1,0:T(8,128)(2,1)S(1)} custom-call(bf16[80,1024]{1,0:T(8,128)(2,1)S(1)} %pad.18.a_ref, bf16[1024,2048]{1,0:T(8,128)(2,1)S(1)} %copy-done.2), custom_call_target="tpu_custom_call" | custom-call | flops 335544320 | bytes 8388608 | tf_op jit(solution)/shard_map/project_and_add/pallas_call | solution.py:410
  172.8 0.7 slice.47
  (59 shorter events, 1.9 us)
Async XLA Ops:
  6.5 2.9 %copy-start = (bf16[2048,512]{1,0:T(8,128)(2,1)S(1)}, bf16[2048,512]{1,0:T(8,128)(2,1)}, u32[]{:S(2)}) copy-start(bf16[2048,512]{1,0:T(8,128)(2,1)} %param.14) | copy-start | bytes 6291460
  6.5 4.4 %copy-start.7 = (bf16[68,2048]{1,0:T(8,128)(2,1)S(1)}, bf16[68,2048]{1,0:T(8,128)(2,1)}, u32[]{:S(2)}) copy-start(bf16[68,2048]{1,0:T(8,128)(2,1)} %param.10) | copy-start | bytes 835588
  6.5 143.9 %all-gather.4.cloned.1.call-start = ((), (), s32[]{:S(2)}) async-start(), calls=%async_computation | async-start | bytes 2506752 | tf_op jit(solution)/shard_map/all_gather | solution.py:493
  7.9 3.1 %copy-start.8 = (bf16[2048,512]{1,0:T(8,128)(2,1)S(1)}, bf16[2048,512]{1,0:T(8,128)(2,1)}, u32[]{:S(2)}) copy-start(bf16[2048,512]{1,0:T(8,128)(2,1)} %param.13) | copy-start | bytes 6291460
  16.0 1.8 %copy-start.10 = (s32[66]{0:T(128)S(1)}, s32[66]{0:T(128)}, u32[]{:S(2)}) copy-start(s32[66]{0:T(128)} %param.18) | copy-start | bytes 796
  57.0 1.7 copy-start.3
  58.7 1.6 copy-start.5
  60.3 1.6 copy-start.6
  69.6 1.4 copy-start.4
  150.5 1.7 copy-start.1
  152.2 5.8 %copy-start.9 = (f32[16,8,128]{2,1,0:T(8,128)S(1)}, f32[16,8,128]{2,1,0:T(8,128)}, u32[]{:S(2)}) copy-start(f32[16,8,128]{2,1,0:T(8,128)} %get-tuple-element.15) | copy-start | bytes 196612
  167.3 2.2 %copy-start.2 = (bf16[1024,2048]{1,0:T(8,128)(2,1)S(1)}, bf16[1024,2048]{1,0:T(8,128)(2,1)}, u32[]{:S(2)}) copy-start(bf16[1024,2048]{1,0:T(8,128)(2,1)} %w_ref.1) | copy-start | bytes 12582916
Sparse Core Ops, SparseCore 0:
  13.0 67.2 all-gather.3

commit v4 on v3

--- a/solution.py
+++ b/solution.py
@@ -118,11 +118,14 @@
 
         @pl.when(hi > lo)
         def _():
+            q = jnp.concatenate(
+                [q_ref[rows, g * HD:(g + 1) * HD] for g in range(groups)], axis=0
+            ).astype(jnp.bfloat16)
+            out, lse = attend(q, lo, hi, lo // TILE, (hi + TILE - 1) // TILE, groups * SPAN)
+            out = out.T.astype(jnp.bfloat16)
             for g in range(groups):
-                q = q_ref[rows, g * HD:(g + 1) * HD].astype(jnp.bfloat16)
-                out, lse = attend(q, lo, hi, lo // TILE, (hi + TILE - 1) // TILE, SPAN)
-                o_ref[rows, g * HD:(g + 1) * HD] = out.T.astype(jnp.bfloat16)
-                l_ref[0, g:g + 1, rows] = lse
+                o_ref[rows, g * HD:(g + 1) * HD] = out[g * SPAN:(g + 1) * SPAN]
+                l_ref[0, g:g + 1, rows] = lse[:, g * SPAN:(g + 1) * SPAN]
 
         @pl.when(hi <= lo)
         def _():
@@ -158,9 +161,9 @@
             pl.BlockSpec((1, groups, rows), lambda c: (c, 0, 0)),
         ),
         scratch_shapes=[
-            pltpu.VMEM((1, SPAN), jnp.float32),
-            pltpu.VMEM((1, SPAN), jnp.float32),
-            pltpu.VMEM((HD, SPAN), jnp.float32),
+            pltpu.VMEM((1, groups * SPAN), jnp.float32),
+            pltpu.VMEM((1, groups * SPAN), jnp.float32),
+            pltpu.VMEM((HD, groups * SPAN), jnp.float32),
             pltpu.VMEM((rows, groups * HD), jnp.float32),
         ],
         compiler_params=pltpu.CompilerParams(vmem_limit_bytes=32 << 20),

time: 177 us -> 192 us (1.085); the launches traced: 180 us -> 189 us
  Pallas kernels: 128 us -> 137 us
    pallas_call x1, Pallas kernels: 73.2 us -> 81.6 us  [exchange(): pl.pallas_call(functools.partial(exchange_kernel, count), name='exchange_...]
  transfers between devices with their start and end apart: 1 -> 1, of which waited for: 0 -> 0; matrix products, arithmetic and copies ran while one was open for 6% -> 6% of each run, Pallas kernels for 66% -> 68%
where the time goes in v4:
time: 192 us; the launch traced here: 189 us
  Pallas kernels  137 us (71%)
  local copies, waits for them, and re-layouts  21.9 us (11%)
  between operations  14.4 us (8%)
  other arithmetic  10.4 us (5%)
  matrix products  5.12 us (3%)
    pallas_call x1, Pallas kernels, exchange(): pl.pallas_call(functools.partial(exchange_kernel, count), name='exchange_...  81.6 us
    pallas_call x1, Pallas kernels, gather(): pl.pallas_call(functools.partial(gather_kernel, bits), name='gather_rows'...  38.5 us
    unnamed x31, local copies, waits for them, and re-layouts  10.4 us
    pallas_call x1, Pallas kernels, cache_attention(): pl.pallas_call(cache_kernel, name='cache_attention', grid=(kv_heads,), ou...  7.67 us
    pallas_call x1, Pallas kernels, self_attention(): pl.pallas_call(self_kernel, name='new_row_attention', grid=(kv_heads,), o...  5.76 us
    reshape x1, local copies, waits for them, and re-layouts, flat_blocks(): values = values.reshape(count, -1, HD)  4.68 us
    reduce_sum x1, other arithmetic, per_device(): cached = jnp.sum(parts.astype(jnp.float32) * weights[..., None], axis=0)  3.93 us
  transfers between devices with their start and end apart: 1, of which 0 were waited for; matrix products, arithmetic and copies ran while one was open for 6% of the time, Pallas kernels for 68%

profile of v4, /device:TPU:15, one launch (start us, length us, event | category | flops | bytes accessed | tf_op | source)
XLA Modules:
  0.0 189.2 jit_solution(8162251372109807804)
XLA Ops:
  6.6 1.3 fusion
  7.9 0.9 select_reduce_fusion.1
  8.8 0.7 convert_element_type.46
  9.5 1.5 convolution_convert_fusion
  11.0 0.5 fusion.8
  11.6 0.2 multiply_cosine_fusion
  11.8 0.2 subtract_convert_fusion.1
  12.2 0.7 maximum_bitcast_fusion
  12.9 3.1 %fusion.10 = f32[68,1024]{1,0:T(8,128)S(1)} fusion(bf16[2048,1024]{1,0:T(8,128)(2,1)} %param.12, bf16[68,2048]{1,0:T(8,128)(2,1)S(1)} %copy-done.7, f32[2048]{0:T(1024)S(1)} %convert_element_type.46, f32[68]{0:T(128)S(1)} %add_rsqrt_fusion), kind=kOutput, calls=%fused_computation.52 | convolution fusion | flops 285769728 | bytes 4759824 | tf_op jit(solution)/shard_map/dot_general | solution.py:482
  16.1 0.2 subtract_convert_fusion
  16.4 0.7 pad.16.x_ref
  18.4 38.5 %gather_rows.1.blocks_ref = bf16[16,80,1024]{2,1,0:T(8,128)(2,1)} custom-call(bf16[80,1024]{1,0:T(8,128)(2,1)} %pad.16.x_ref), custom_call_target="tpu_custom_call" | custom-call | bytes 104857600 | tf_op jit(solution)/shard_map/gather_rows/pallas_call | solution.py:296
  57.0 1.7 copy-done.3
  58.7 1.6 copy-done.5
  60.3 1.6 copy-done.6
  61.9 7.7 %cache_attention.1 = (bf16[1088,1024]{1,0:T(8,128)(2,1)S(1)}, f32[4,2,1088]{2,1,0:T(2,128)S(1)}) custom-call(s32[4]{0:T(128)S(1)} %reshape.213.range_ref, s32[1,128]{1,0:T(1,128)S(1)} %broadcast_in_dim_tile.6.lo_ref, s32[1,128]{1,0:T(1,128)S(1)} %broadcast_in_dim_tile.7.hi_ref, bf16[16,80,1024]{2,1,0:T(8,128)(2,1)S(1)} %copy-done.3, ...), custom_call_target="tpu_custom_call" | custom-call | flops 4294967296 | bytes 8388608 | tf_op jit(solution)/shard_map/cache_attention/pallas_call | solution.py:143
  69.6 1.3 copy-done.4
  70.9 4.7 %reshape.214.x_ref = bf16[16,544,128]{2,1,0:T(8,128)(2,1)} reshape(bf16[1088,1024]{1,0:T(8,128)(2,1)} %copy-done.4) | data formatting | bytes 4456448 | tf_op jit(solution)/shard_map/reshape | solution.py:435
  75.8 0.6 pad.17.l_ref
  76.4 81.6 %exchange_partials.1 = (bf16[16,544,128]{2,1,0:T(8,128)(2,1)}, f32[16,8,128]{2,1,0:T(8,128)}) custom-call(bf16[16,544,128]{2,1,0:T(8,128)(2,1)} %reshape.214.x_ref, f32[16,8,128]{2,1,0:T(8,128)} %pad.17.l_ref), custom_call_target="tpu_custom_call" | custom-call | bytes 167772160 | tf_op jit(solution)/shard_map/exchange_partials/pallas_call | solution.py:345
  158.0 0.9 bitcast_reduce_fusion
  158.9 1.7 copy-done.1
  160.6 5.8 %new_row_attention.1 = (f32[128,1024]{1,0:T(8,128)S(1)}, f32[4,2,128]{2,1,0:T(2,128)S(1)}) custom-call(s32[1,128]{1,0:T(1,128)S(1)} %get-tuple-element.31.lo_ref, s32[1,128]{1,0:T(1,128)S(1)} %get-tuple-element.32.hi_ref, bf16[128,1024]{1,0:T(8,128)(2,1)S(1)} %pad.15.q_ref, bf16[16,68,1024]{2,1,0:T(8,128)(2,1)S(1)} %copy-done.1, ...), custom_call_target="tpu_custom_call" | custom-call | flops 570425344 | bytes 4194304 | tf_op jit(solution)/shard_map/new_row_attention/pallas_call | solution.py:201
  166.6 0.1 mul.169
  167.1 0.9 copy.29
  167.9 1.1 copy.30
  169.0 3.9 %multiply_reduce_fusion = f32[544,128]{1,0:T(8,128)} fusion(bf16[16,544,128]{2,1,0:T(8,128)(2,1)} %get-tuple-element.16, f32[16,544]{1,0:T(8,128)S(1)} %copy.30), kind=kLoop, calls=%fused_computation | loop fusion | flops 3272704 | bytes 2541568 | tf_op jit(solution)/shard_map/reduce_sum | solution.py:528
  172.9 1.7 reduce_sum.51
  174.7 1.0 divide_convert_fusion
  175.7 2.2 %copy-done.2 = bf16[1024,2048]{1,0:T(8,128)(2,1)S(1)} copy-done((bf16[1024,2048]{1,0:T(8,128)(2,1)S(1)}, bf16[1024,2048]{1,0:T(8,128)(2,1)}, u32[]{:S(2)}) %copy-start.2) | copy-done | bytes 4194328
  177.9 3.8 %project_and_add.1 = bf16[80,1024]{1,0:T(8,128)(2,1)S(1)} custom-call(bf16[80,1024]{1,0:T(8,128)(2,1)S(1)} %pad.18.a_ref, bf16[1024,2048]{1,0:T(8,128)(2,1)S(1)} %copy-done.2), custom_call_target="tpu_custom_call" | custom-call | flops 335544320 | bytes 8388608 | tf_op jit(solution)/shard_map/project_and_add/pallas_call | solution.py:413
  181.7 0.7 slice.47
  (59 shorter events, 1.9 us)
Async XLA Ops:
  6.5 2.9 %copy-start = (bf16[2048,512]{1,0:T(8,128)(2,1)S(1)}, bf16[2048,512]{1,0:T(8,128)(2,1)}, u32[]{:S(2)}) copy-start(bf16[2048,512]{1,0:T(8,128)(2,1)} %param.14) | copy-start | bytes 6291460
  6.5 4.4 %copy-start.7 = (bf16[68,2048]{1,0:T(8,128)(2,1)S(1)}, bf16[68,2048]{1,0:T(8,128)(2,1)}, u32[]{:S(2)}) copy-start(bf16[68,2048]{1,0:T(8,128)(2,1)} %param.10) | copy-start | bytes 835588
  6.5 152.4 %all-gather.4.cloned.1.call-start = ((), (), s32[]{:S(2)}) async-start(), calls=%async_computation | async-start | bytes 2506752 | tf_op jit(solution)/shard_map/all_gather | solution.py:496
  7.9 3.1 %copy-start.8 = (bf16[2048,512]{1,0:T(8,128)(2,1)S(1)}, bf16[2048,512]{1,0:T(8,128)(2,1)}, u32[]{:S(2)}) copy-start(bf16[2048,512]{1,0:T(8,128)(2,1)} %param.13) | copy-start | bytes 6291460
  16.0 1.8 copy-start.10
  57.0 1.7 copy-start.3
  58.7 1.6 copy-start.5
  60.3 1.6 copy-start.6
  69.6 1.4 copy-start.4
  158.9 1.7 copy-start.1
  160.6 5.8 %copy-start.9 = (f32[16,8,128]{2,1,0:T(8,128)S(1)}, f32[16,8,128]{2,1,0:T(8,128)}, u32[]{:S(2)}) copy-start(f32[16,8,128]{2,1,0:T(8,128)} %get-tuple-element.15) | copy-start | bytes 196612
  175.7 2.2 %copy-start.2 = (bf16[1024,2048]{1,0:T(8,128)(2,1)S(1)}, bf16[1024,2048]{1,0:T(8,128)(2,1)}, u32[]{:S(2)}) copy-start(bf16[1024,2048]{1,0:T(8,128)(2,1)} %w_ref.1) | copy-start | bytes 12582916
Sparse Core Ops, SparseCore 0:
  13.0 67.2 all-gather.3
